TPU v7x, 512 devices: a whole 4x4x16 slice. The times are simulated.
512 devices in a mesh: cls: 128 (over x, z, core), smp: 4 (over y).
Axes of the slice: x: 4, y: 4, z: 16, core: 2. Of those that a mesh axis runs over, the one named last changes fastest.
Arguments:
- counts: float32 [64, 131072], P('smp', 'cls'), may hold values from 0.1 to 300, as said below
- compat: bfloat16 [1024, 4, 128, 128], P('cls'), may hold values from 0.0099487305 to 1
- link_owner: int32 [1024, 4], P('cls'), may hold values from 0 to 127, all different within a row; in each aligned block of 8 rows (0 to 7, 8 to 15, ...) at most 2 rows name the same one
- link_local: int32 [1024, 4], P('cls'), may hold values from 0 to 3
- start: float32 [64, 65536], P('smp', 'cls'), may hold values from 0.2 to 5
Outputs:
- abundance: float32 [64, 65536], P('smp', 'cls')
Inputs may be any that keep to these rules, and one draw needn't show every extreme that they name: `link_owner`: among the links of the class tiles of one index of cls, no owner is named more than 2 times, a bound that some block reaches; the 4 owners of one class tile differ. `counts`: Positive.
All inputs are finite; a program needn't handle non-finite values.
Results may differ from a plain program's by a relative error of at most 0.00048.
Values may be sent and summed in bfloat16 or wider, within the bound.
A program may use at most 64 MiB of HBM per device.

v0:
```python
import jax
import jax.numpy as jnp
from jax import lax
from jax.sharding import PartitionSpec as P

TILE = 128
K = 4
ITERS = 3


MIXING = 0.3


def body(counts, compat, link_owner, link_local, start):
    owner_count = lax.axis_size("cls")
    sample_parts = lax.axis_size("smp")
    samples_dev, columns = start.shape
    tiles_dev = columns // TILE
    ctiles = compat.shape[0]
    link_count = ctiles * K
    capacity = max(2, (2 * link_count + owner_count - 1) // owner_count)
    owners = link_owner.reshape(-1)
    local_tile = link_local.reshape(-1)
    owner_hits = (owners[:, None] == jnp.arange(owner_count, dtype=jnp.int32)[None, :]).astype(
        jnp.int32
    )
    slot_rank = jnp.sum((jnp.cumsum(owner_hits, axis=0) - 1) * owner_hits, axis=1)
    slot_of = owners * capacity + slot_rank
    request = jnp.full((owner_count * capacity,), -1, jnp.int32).at[slot_of].set(local_tile)
    wanted = lax.all_to_all(
        request.reshape(owner_count, capacity), "cls", split_axis=0, concat_axis=0, tiled=True
    ).reshape(-1)
    picker = (wanted[:, None] == jnp.arange(tiles_dev, dtype=jnp.int32)[None, :]).astype(
        jnp.bfloat16
    )
    sample_total = lax.psum(jnp.sum(counts, axis=1), "cls")
    class_counts = counts.reshape(samples_dev, ctiles, TILE)
    theta = start
    for sweep in range(ITERS):
        theta_b = theta.astype(jnp.bfloat16)
        outgoing = jnp.einsum(
            "jt,stb->jsb",
            picker,
            theta_b.reshape(samples_dev, tiles_dev, TILE),
            preferred_element_type=jnp.float32,
        ).astype(jnp.bfloat16)
        incoming = lax.all_to_all(
            outgoing.reshape(owner_count, capacity, samples_dev, TILE),
            "cls",
            split_axis=0,
            concat_axis=0,
            tiled=True,
        )
        incoming = incoming.reshape(owner_count * capacity, samples_dev, TILE)
        fetched = jnp.take(incoming, slot_of, axis=0).reshape(ctiles, K, samples_dev, TILE)
        expected = jnp.einsum("ikab,iksb->sia", compat, fetched, preferred_element_type=jnp.float32)
        class_ratio = (class_counts / expected).astype(jnp.bfloat16)
        share = jnp.einsum(
            "sia,ikab->iksb", class_ratio, compat, preferred_element_type=jnp.float32
        ).astype(jnp.bfloat16)
        share = share.reshape(link_count, samples_dev, TILE)
        outbox = (
            jnp.zeros((owner_count * capacity, samples_dev, TILE), jnp.bfloat16)
            .at[slot_of]
            .set(share)
        )
        arrived = lax.all_to_all(
            outbox.reshape(owner_count, capacity, samples_dev, TILE),
            "cls",
            split_axis=0,
            concat_axis=0,
            tiled=True,
        )
        arrived = arrived.reshape(owner_count * capacity, samples_dev, TILE)
        returned = jnp.einsum(
            "jt,jsb->stb", picker, arrived, preferred_element_type=jnp.float32
        ).reshape(samples_dev, columns)
        updated = theta * returned / sample_total[:, None]
        pooled = lax.psum(jnp.sum(updated, axis=0), "smp") / (samples_dev * sample_parts)
        theta = (1.0 - MIXING) * updated + MIXING * pooled[None, :]
    return theta * (columns * owner_count)


def solution(mesh):
    placed = (
        P("smp", "cls"),
        P("cls", None, None, None),
        P("cls", None),
        P("cls", None),
        P("smp", "cls"),
    )
    return jax.shard_map(
        body, mesh=mesh, in_specs=placed, out_specs=P("smp", "cls"), check_vma=False
    )
```

profile of v0, /device:TPU:1, one launch (start us, length us, event | category | flops | bytes accessed | tf_op | source)
XLA Modules:
  0.0 693.9 jit_solution(8293061655595441737)
XLA Ops:
  0.0 0.8 broadcast_multiply_fusion.3
  0.8 0.8 copy.41
  1.7 0.8 copy.42
  2.7 0.2 select_reduce_fusion
  2.9 0.7 scatter_custom_fusion
  3.6 0.8 all_to_all.24
  4.4 20.4 %all-to-all-start = ((s32[128,1,2]{2,1,0:T(1,128)}), s32[128,1,2]{2,1,0:T(1,128)S(1)}, u32[]{:S(2)}, u32[]{:S(2)}) async-start(s32[128,1,2]{2,1,0:T(1,128)} %bitcast.2), calls=%async_computation | async-start | bytes 131072 | tf_op jit(solution)/shard_map/all_to_all | solution.py:30
  24.8 0.8 convert_element_type.50
  25.6 14.2 %all-to-all-done = s32[128,1,2]{2,1,0:T(1,128)S(1)} async-done(((s32[128,1,2]{2,1,0:T(1,128)}), s32[128,1,2]{2,1,0:T(1,128)S(1)}, u32[]{:S(2)}, u32[]{:S(2)}) %all-to-all-start) | async-done | bytes 1056 | tf_op jit(solution)/shard_map/all_to_all | solution.py:30
  39.8 0.5 broadcast.85
  40.3 0.8 reduce.3
  41.2 0.5 convolution_convert_fusion.2
  41.8 1.7 copy.44
  43.5 6.6 all-to-all-start.1
  50.2 54.4 %all-to-all-done.1 = bf16[128,2,16,128]{3,1,2,0:T(2,128)(2,1)S(1)} async-done(((bf16[128,2,16,128]{3,1,2,0:T(2,128)(2,1)}), bf16[128,2,16,128]{3,1,2,0:T(2,128)(2,1)S(1)}, u32[]{:S(2)}, u32[]{:S(2)}) %all-to-all-start.1) | async-done | bytes 1048608 | tf_op jit(solution)/shard_map/all_to_all | solution.py:47
  104.8 0.6 gather_fusion
  105.5 0.5 convolution_convert_fusion.5
  106.2 1.5 scatter_fusion
  107.7 1.8 copy.47
  109.5 8.5 %all-to-all-start.2 = ((bf16[128,2,16,128]{3,1,2,0:T(2,128)(2,1)}), bf16[128,2,16,128]{3,1,2,0:T(2,128)(2,1)S(1)}, u32[]{:S(2)}, u32[]{:S(2)}) async-start(bf16[128,2,16,128]{3,1,2,0:T(2,128)(2,1)} %copy.47), calls=%async_computation.2 | async-start | bytes 2097152 | tf_op jit(solution)/shard_map/all_to_all | solution.py:67
  118.1 286.6 %psum.28 = f32[16]{0:T(128)S(1)} all-reduce(f32[16]{0:T(128)S(1)} %reduce_sum.49), channel_id=1, replica_groups=mesh['cls'=128,'smp'=4] {'cls'}, use_global_device_ids=true, to_apply=%region_5.7 | all-reduce | flops 16 | bytes 128 | tf_op jit(solution)/shard_map/psum | solution.py:36
  404.7 1.0 copy.48
  405.7 0.2 fusion.31
  406.0 0.5 copy-done.2
  406.6 8.9 %psum.29 = f32[512]{0:T(512)S(1)} all-reduce(f32[512]{0:T(512)S(1)} %get-tuple-element.10), channel_id=1, replica_groups=mesh['cls'=128,'smp'=4] {'smp'}, use_global_device_ids=true, to_apply=%region_7.9 | all-reduce | flops 512 | bytes 4096 | tf_op jit(solution)/shard_map/psum | solution.py:79
  415.5 0.5 convolution_convert_fusion.1
  416.0 0.7 copy.49
  416.8 61.2 %all_to_all.39 = bf16[128,2,16,128]{3,1,2,0:T(2,128)(2,1)S(1)} all-to-all(bf16[128,2,16,128]{3,1,2,0:T(2,128)(2,1)S(1)} %copy.49), channel_id=1, replica_groups=mesh['cls'=128,'smp'=4] {'cls'}, dimensions={0} | all-to-all | bytes 2097152 | tf_op jit(solution)/shard_map/all_to_all | solution.py:47
  478.1 0.6 gather_fusion.1
  478.8 0.5 convolution_convert_fusion.4
  479.5 1.5 scatter_fusion.1
  481.0 0.8 copy.52
  481.9 62.6 %all_to_all.40 = bf16[128,2,16,128]{3,1,2,0:T(2,128)(2,1)S(1)} all-to-all(bf16[128,2,16,128]{3,1,2,0:T(2,128)(2,1)S(1)} %copy.52), channel_id=1, replica_groups=mesh['cls'=128,'smp'=4] {'cls'}, dimensions={0} | all-to-all | bytes 2097152 | tf_op jit(solution)/shard_map/all_to_all | solution.py:67
  544.5 1.0 copy.53
  545.5 0.2 fusion.28
  545.8 6.0 psum.30
  551.8 0.5 convolution_convert_fusion
  552.4 0.7 copy.54
  553.1 64.4 %all_to_all.41 = bf16[128,2,16,128]{3,1,2,0:T(2,128)(2,1)S(1)} all-to-all(bf16[128,2,16,128]{3,1,2,0:T(2,128)(2,1)S(1)} %copy.54), channel_id=1, replica_groups=mesh['cls'=128,'smp'=4] {'cls'}, dimensions={0} | all-to-all | bytes 2097152 | tf_op jit(solution)/shard_map/all_to_all | solution.py:47
  617.6 0.6 gather_fusion.2
  618.3 0.5 convolution_convert_fusion.3
  619.0 1.5 scatter_fusion.2
  620.5 0.8 copy.57
  621.4 62.6 %all_to_all.42 = bf16[128,2,16,128]{3,1,2,0:T(2,128)(2,1)S(1)} all-to-all(bf16[128,2,16,128]{3,1,2,0:T(2,128)(2,1)S(1)} %copy.57), channel_id=1, replica_groups=mesh['cls'=128,'smp'=4] {'cls'}, dimensions={0} | all-to-all | bytes 2097152 | tf_op jit(solution)/shard_map/all_to_all | solution.py:67
  684.0 1.0 copy.58
  685.0 0.2 fusion.25
  685.3 7.9 %psum.31 = f32[512]{0:T(512)S(1)} all-reduce(f32[512]{0:T(512)S(1)} %get-tuple-element.6), channel_id=1, replica_groups=mesh['cls'=128,'smp'=4] {'smp'}, use_global_device_ids=true, to_apply=%region_13.15 | all-reduce | flops 512 | bytes 4096 | tf_op jit(solution)/shard_map/psum | solution.py:79
  693.3 0.6 add_multiply_fusion
  (37 shorter events, 2.4 us)
Async XLA Ops:
  0.0 105.5 %copy-start = (bf16[8,4,128,128]{3,2,1,0:T(8,128)(2,1)S(1)}, bf16[8,4,128,128]{3,2,1,0:T(8,128)(2,1)}, u32[]{:S(2)}) copy-start(bf16[8,4,128,128]{3,2,1,0:T(8,128)(2,1)} %param.8) | copy-start | bytes 3145732
  4.4 35.4 %all-to-all-start = ((s32[128,1,2]{2,1,0:T(1,128)}), s32[128,1,2]{2,1,0:T(1,128)S(1)}, u32[]{:S(2)}, u32[]{:S(2)}) async-start(s32[128,1,2]{2,1,0:T(1,128)} %bitcast.2), calls=%async_computation | async-start | bytes 131072 | tf_op jit(solution)/shard_map/all_to_all | solution.py:30
  43.5 61.1 %all-to-all-start.1 = ((bf16[128,2,16,128]{3,1,2,0:T(2,128)(2,1)}), bf16[128,2,16,128]{3,1,2,0:T(2,128)(2,1)S(1)}, u32[]{:S(2)}, u32[]{:S(2)}) async-start(bf16[128,2,16,128]{3,1,2,0:T(2,128)(2,1)} %copy.44), calls=%async_computation.1 | async-start | bytes 2097152 | tf_op jit(solution)/shard_map/all_to_all | solution.py:47
  50.2 55.3 %copy-start.1 = (f32[16,1024]{1,0:T(8,128)S(1)}, f32[16,1024]{1,0:T(8,128)}, u32[]{:S(2)}) copy-start(f32[16,1024]{1,0:T(8,128)} %param.7) | copy-start | bytes 196612
  109.5 295.2 %all-to-all-start.2 = ((bf16[128,2,16,128]{3,1,2,0:T(2,128)(2,1)}), bf16[128,2,16,128]{3,1,2,0:T(2,128)(2,1)S(1)}, u32[]{:S(2)}, u32[]{:S(2)}) async-start(bf16[128,2,16,128]{3,1,2,0:T(2,128)(2,1)} %copy.47), calls=%async_computation.2 | async-start | bytes 2097152 | tf_op jit(solution)/shard_map/all_to_all | solution.py:67
  405.7 0.8 copy-start.2
where the time goes:
time: 697 us; the launch traced here: 694 us
  blocking collectives  560 us (80%)
  waiting for transfers between devices  68.6 us (10%)
  starting transfers between devices  35.5 us (5%)
  local copies, waits for them, and re-layouts  21.3 us (3%)
    psum x1, blocking collectives, body(): sample_total = lax.psum(jnp.sum(counts, axis=1), 'cls')  287 us
    all_to_all x2, blocking collectives, body(): lax.all_to_all(outgoing.reshape(owner_count, capacity, samples_dev, TILE)...  126 us
    all_to_all x2, blocking collectives, body(): lax.all_to_all(outbox.reshape(owner_count, capacity, samples_dev, TILE),...  125 us
    all_to_all x1, waiting for transfers between devices, body(): lax.all_to_all(outgoing.reshape(owner_count, capacity, samples_dev, TILE)...  54.4 us
    psum x3, blocking collectives, body(): lax.psum(jnp.sum(updated, axis=0), 'smp') / (samples_dev * sample_parts)  22.9 us
    all_to_all x1, starting transfers between devices, body(): lax.all_to_all(request.reshape(owner_count, capacity), 'cls', split_axis=...  20.4 us
    all_to_all x1, waiting for transfers between devices, body(): lax.all_to_all(request.reshape(owner_count, capacity), 'cls', split_axis=...  14.2 us
  transfers between devices with their start and end apart: 3, of which 2 were waited for; matrix products, arithmetic and copies ran while one was open for 0% of the time, Pallas kernels for 0%

commit v1 on v0

v1 whole, which is shorter than its diff:
```python
import functools

import jax
import jax.numpy as jnp
from jax import lax
from jax.experimental import pallas as pl
from jax.experimental.pallas import tpu as pltpu
from jax.sharding import PartitionSpec as P

TILE = 128
K = 4
ITERS = 3
MIXING = 0.3
MESH = pl.DeviceIdType.MESH
NX, NZ, NC, NY = 4, 16, 2, 4
TD = 4
LINKS = 32
COL = NZ * NC * TD
HALF = NZ * TD
STEP = 5
NEAR = (1, -1, 2, -2)


def em_kernel(
    tid, perm, keep, pos, counts, compat, start, out,
    th, xs, xr, sr, cum, d, cr, nr, sf, fr, tt, tx, tot, ps, theta,
    fz_s, fz_r, fc_s, fc_r, fx_s, fx_r, rx_s, rx_r, rc_s, rc_r,
    rn_s, rn_r, rf_s, rf_r, tz_s, tz_r, tg_s, tg_r, p_s, p_r,
):
    me = lax.axis_index("cls")
    y = lax.axis_index("smp")
    c = me % NC
    z = (me // NC) % NZ
    x = me // (NC * NZ)

    def zrel(off):
        return (z + off + NZ) % NZ

    def at(dx=0, dz=0, dc=0, dy=0):
        return (
            ((((x + dx) % NX) * NZ + zrel(dz)) * NC + (c + dc) % NC),
            (y + dy) % NY,
        )

    def copy(src, dst, send, recv, dev):
        return pltpu.make_async_remote_copy(
            src_ref=src, dst_ref=dst, send_sem=send, recv_sem=recv,
            device_id=dev, device_id_type=MESH,
        )

    peers = [dict(dz=o) for o in (1, -1, 2, -2, 3, -3, STEP, -STEP)]
    peers += [dict(dc=1)] + [dict(dx=o) for o in (1, 2, 3)] + [dict(dy=o) for o in (1, 2, 3)]
    group = [(dx, dc) for dx in range(NX) for dc in range(NC) if (dx, dc) != (0, 0)]
    peers += [dict(dx=dx, dc=1) for dx in (1, 2, 3)]
    barrier = pltpu.get_barrier_semaphore()
    for peer in peers:
        pl.semaphore_signal(barrier, inc=1, device_id=at(**peer), device_id_type=MESH)
    pl.semaphore_wait(barrier, len(peers))

    far = [(0, 0, STEP), (1, 0, -STEP)]
    near_own = [(2 + j, 0, o) for j, o in enumerate(NEAR)]
    near_low = [(6 + j, -STEP, o) for j, o in enumerate(NEAR)] + [(10, -STEP, 3)]
    near_high = [(11 + j, STEP, o) for j, o in enumerate(NEAR)]
    every = far + near_own + near_low + near_high

    def spread(blk, send, recv, arrived):
        def move(k, off, way):
            ref = blk(zrel(off))
            return copy(ref, ref, send.at[k], recv.at[k], at(dz=way))

        def take(k, off, way):
            ref = blk(zrel(off - way))
            copy(ref, ref, send.at[k], recv.at[k], at(dz=way)).wait_recv()
            arrived(1 + k, off - way)

        def first():
            for k, off, way in far + near_own:
                move(k, off, way).start()
            arrived(0, 0)

        def second():
            take(*far[0])
            for step in near_low:
                move(*step).start()
            take(*far[1])
            for step in near_high:
                move(*step).start()

        def third():
            for step in near_own + near_low + near_high:
                take(*step)

        def close():
            for step in every:
                move(*step).wait_send()

        return first, second, third, close

    def th_blk(core):
        def ref(zz):
            return th.at[pl.ds((zz * NC + core) * TD, TD)]

        return ref

    def to_core(k, off, mine=True):
        ref = th_blk(c if mine else 1 - c)(zrel(off))
        return copy(ref, ref, fc_s.at[k], fc_r.at[k], at(dc=1))

    f_first, f_second, f_third, f_close = spread(
        th_blk(c), fz_s, fz_r, lambda k, off: to_core(k, off).start()
    )
    core_steps = [(0, 0)] + [(1 + k, off - way) for k, off, way in every]
    t_first, t_second, t_third, t_close = spread(
        lambda zz: tt.at[zz], tz_s, tz_r, lambda k, off: None
    )

    theta[...] = start[...]
    cum[COL] = jnp.zeros((16, TILE), jnp.float32)

    def total_own():
        s = counts[:, 0:TILE]
        for i in range(1, counts.shape[1] // TILE):
            s = s + counts[:, i * TILE : (i + 1) * TILE]
        tt[z] = s

    def tg(j, dx, dc):
        return copy(tx.at[0], tx.at[1 + j], tg_s.at[j], tg_r.at[j], at(dx=dx, dc=dc))

    def sweep(r, carry):
        for t in range(TD):
            th[(z * NC + c) * TD + t] = theta[:, t * TILE : (t + 1) * TILE].astype(jnp.bfloat16)
        f_first()

        @pl.when(r == 0)
        def _():
            total_own()
            t_first()

        f_second()

        @pl.when(r == 0)
        def _():
            t_second()

        f_third()
        for k, off in core_steps:
            to_core(k, off, mine=False).wait_recv()

        def xcopy(dx):
            return copy(
                xs.at[pl.ds((dx - 1) * LINKS, LINKS)],
                xr.at[pl.ds(x * LINKS, LINKS)],
                fx_s.at[dx - 1],
                fx_r.at[dx - 1],
                at(dx=dx),
            )

        for dx in (2, 1, 3):
            row = ((x + dx) % NX) * LINKS

            def pick(l, _, dx=dx, row=row):
                xs[(dx - 1) * LINKS + l] = th[tid[row + l] % COL]
                return 0

            lax.fori_loop(0, LINKS, pick, 0, unroll=8)
            xcopy(dx).start()

        def pick_own(l, _):
            xr[x * LINKS + l] = th[tid[x * LINKS + l] % COL]
            return 0

        lax.fori_loop(0, LINKS, pick_own, 0, unroll=8)

        @pl.when(r == 0)
        def _():
            t_third()
            s = tt[0]
            for i in range(1, NZ):
                s = s + tt[i]
            tx[0] = s
            for j, (dx, dc) in enumerate(group):
                tg(j, dx, dc).start()

        def xwait(dx):
            ref = xr.at[pl.ds(((x + NX - dx) % NX) * LINKS, LINKS)]
            copy(ref, ref, fx_s.at[dx - 1], fx_r.at[dx - 1], at(dx=dx)).wait_recv()

        for dx in (1, 3, 2):
            xwait(dx)

        def tile(i, _):
            acc = jnp.zeros((16, TILE), jnp.float32)
            for k in range(K):
                l = i * K + k
                got = xr[(tid[x * LINKS + l] // COL) * LINKS + l]
                acc = acc + lax.dot_general(
                    got, compat[i, k], (((1,), (1,)), ((), ())),
                    preferred_element_type=jnp.float32,
                )
            ratio = (counts[:, pl.ds(pl.multiple_of(i * TILE, TILE), TILE)] / acc).astype(
                jnp.bfloat16
            )
            for k in range(K):
                sr[x * LINKS + i * K + k] = jnp.dot(
                    ratio, compat[i, k], preferred_element_type=jnp.float32
                ).astype(jnp.bfloat16)
            return 0

        lax.fori_loop(0, LINKS // K, tile, 0, unroll=2)

        def scopy(dx, src_x):
            ref = sr.at[pl.ds(src_x * LINKS, LINKS)]
            return copy(ref, ref, rx_s.at[dx - 1], rx_r.at[dx - 1], at(dx=dx))

        for dx in (2, 1, 3):
            scopy(dx, x).start()
        f_close()
        for k, off in core_steps:
            to_core(k, off).wait_send()
        for dx in (1, 3, 2):
            scopy(dx, (x + NX - dx) % NX).wait_recv()

        def add(j, acc):
            acc = jnp.where(keep[j] > 0, acc, 0.0) + sr[perm[j]].astype(jnp.float32)
            cum[j] = acc
            return acc

        lax.fori_loop(0, COL, add, jnp.zeros((16, TILE), jnp.float32), unroll=8)

        def dense(core):
            def one(i, _):
                for t in range(TD):
                    g = (i * NC + core) * TD + t
                    d[core * HALF + i * TD + t] = cum[pos[g]]
                return 0

            lax.fori_loop(0, NZ, one, 0, unroll=4)

        dense(1 - c)
        rcopy = copy(
            d.at[pl.ds((1 - c) * HALF, HALF)], cr, rc_s.at[0], rc_r.at[0], at(dc=1)
        )
        rcopy.start()
        dense(c)
        rcopy.wait_recv()

        def join(i, _):
            d[c * HALF + i] = d[c * HALF + i] + cr[i]
            return 0

        lax.fori_loop(0, HALF, join, 0, unroll=8)

        def dz(off):
            return d.at[pl.ds(c * HALF + zrel(off) * TD, TD)]

        kinds = (0, STEP, -STEP)
        nsteps = [
            (j * 3 + k, way, way + kind)
            for j, way in enumerate(NEAR)
            for k, kind in enumerate(kinds)
        ] + [(12, 3, 8)]

        def ncopy(slot, way, dest):
            return copy(
                dz(dest), nr.at[pl.ds(slot * TD, TD)], rn_s.at[slot], rn_r.at[slot], at(dz=way)
            )

        def fcopy(j, way):
            return copy(
                sf.at[pl.ds(j * TD, TD)], fr.at[pl.ds(j * TD, TD)], rf_s.at[j], rf_r.at[j],
                at(dz=way),
            )

        order = [n for n in nsteps if n[0] % 3 or n[0] == 12] + [
            n for n in nsteps if n[0] % 3 == 0 and n[0] != 12
        ]
        for n in order:
            ncopy(*n).start()
        for j, kind in ((0, STEP), (1, -STEP)):
            slots = [jj * 3 + 1 + j for jj in range(4)] + ([12] if j == 0 else [])
            for n in nsteps:
                if n[0] in slots:
                    ncopy(*n).wait_recv()
            for t in range(TD):
                acc = d[c * HALF + zrel(kind) * TD + t]
                for s in slots:
                    acc = acc + nr[s * TD + t]
                sf[j * TD + t] = acc
            fcopy(j, kind).start()
        own = [jj * 3 for jj in range(4)]
        for n in nsteps:
            if n[0] in own:
                ncopy(*n).wait_recv()

        @pl.when(r == 0)
        def _():
            for j, (dx, dc) in enumerate(group):
                tg(j, dx, dc).wait_recv()
            s = tx[0]
            for j in range(len(group)):
                s = s + tx[1 + j]
            tot[...] = jnp.broadcast_to(jnp.sum(s, axis=1, keepdims=True), (16, TILE))

        fcopy(0, STEP).wait_recv()
        fcopy(1, -STEP).wait_recv()
        for t in range(TD):
            acc = d[c * HALF + z * TD + t]
            for s in own:
                acc = acc + nr[s * TD + t]
            acc = acc + (fr[t] + fr[TD + t])
            cols = slice(t * TILE, (t + 1) * TILE)
            updated = theta[:, cols] * acc / tot[...]
            theta[:, cols] = updated
            ps[r * NY, :, cols] = jnp.sum(updated, axis=0, keepdims=True)

        def pcopy(dy):
            return copy(ps.at[r * NY], ps.at[r * NY + dy], p_s.at[r * 3 + dy - 1],
                        p_r.at[r * 3 + dy - 1], at(dy=dy))

        for dy in (2, 1, 3):
            pcopy(dy).start()
        for dx in (1, 2, 3):
            xcopy(dx).wait_send()
            scopy(dx, x).wait_send()
        rcopy.wait_send()
        for n in nsteps:
            ncopy(*n).wait_send()
        fcopy(0, STEP).wait_send()
        fcopy(1, -STEP).wait_send()

        @pl.when(r == 0)
        def _():
            t_close()
            for j, (dx, dc) in enumerate(group):
                tg(j, dx, dc).wait_send()

        for dy in (1, 3, 2):
            pcopy(dy).wait_recv()
        pooled = ps[r * NY] + ps[r * NY + 1] + ps[r * NY + 2] + ps[r * NY + 3]
        theta[...] = (1.0 - MIXING) * theta[...] + (MIXING / (16 * NY)) * pooled
        for dy in (1, 2, 3):
            pcopy(dy).wait_send()
        return carry

    lax.fori_loop(0, ITERS, sweep, 0)
    out[...] = theta[...] * 65536.0


def body(counts, compat, link_owner, link_local, start):
    x = lax.axis_index("cls") // (NZ * NC)
    mine = (link_owner * TD + link_local).reshape(-1)
    groups = [[(i * NZ + j) * NC + k for i in range(NX)] for j in range(NZ) for k in range(NC)]
    tid = lax.all_gather(mine, "cls", axis_index_groups=groups, tiled=True)
    key = jnp.where(tid // COL == x, tid % COL, COL)
    order = jnp.arange(COL, dtype=jnp.int32)
    before = (key[None, :] < key[:, None]) | (
        (key[None, :] == key[:, None]) & (order[None, :] < order[:, None])
    )
    rank = jnp.sum(before.astype(jnp.int32), axis=1)
    place = rank[None, :] == order[:, None]
    perm = jnp.sum(jnp.where(place, order[None, :], 0), axis=1)
    skey = jnp.sum(jnp.where(place, key[None, :], 0), axis=1)
    keep = jnp.concatenate(
        [jnp.zeros((1,), jnp.int32), (skey[1:] == skey[:-1]).astype(jnp.int32)]
    )
    upto = jnp.sum((key[None, :] <= order[:, None]).astype(jnp.int32), axis=1)
    some = jnp.any(key[None, :] == order[:, None], axis=1)
    pos = jnp.where(some, upto - 1, COL)
    smem = pl.BlockSpec(memory_space=pltpu.SMEM)
    vmem = pl.BlockSpec(memory_space=pltpu.VMEM)
    f32, bf16 = jnp.float32, jnp.bfloat16
    dma = pltpu.SemaphoreType.DMA

    def buf(n, dtype):
        return pltpu.VMEM((n, 16, TILE), dtype)

    return pl.pallas_call(
        em_kernel,
        out_shape=jax.ShapeDtypeStruct(start.shape, f32),
        in_specs=[smem] * 4 + [vmem] * 3,
        out_specs=vmem,
        scratch_shapes=[
            buf(COL, bf16),
            buf(3 * LINKS, bf16),
            buf(NX * LINKS, bf16),
            buf(NX * LINKS, bf16),
            buf(COL + 1, f32),
            buf(COL, f32),
            buf(HALF, f32),
            buf(13 * TD, f32),
            buf(2 * TD, f32),
            buf(2 * TD, f32),
            buf(NZ, f32),
            buf(NX * NC, f32),
            pltpu.VMEM((16, TILE), f32),
            pltpu.VMEM((ITERS * NY, 1, TD * TILE), f32),
            pltpu.VMEM((16, TD * TILE), f32),
            dma((15,)), dma((15,)),
            dma((16,)), dma((16,)),
            dma((3,)), dma((3,)),
            dma((3,)), dma((3,)),
            dma((1,)), dma((1,)),
            dma((13,)), dma((13,)),
            dma((2,)), dma((2,)),
            dma((15,)), dma((15,)),
            dma((7,)), dma((7,)),
            dma((9,)), dma((9,)),
        ],
        compiler_params=pltpu.CompilerParams(
            collective_id=0, has_side_effects=True, vmem_limit_bytes=40 << 20
        ),
        name="em_rounds",
    )(tid, perm, keep, pos, counts, compat, start)


def solution(mesh):
    placed = (
        P("smp", "cls"),
        P("cls", None, None, None),
        P("cls", None),
        P("cls", None),
        P("smp", "cls"),
    )
    return jax.shard_map(
        body, mesh=mesh, in_specs=placed, out_specs=P("smp", "cls"), check_vma=False
    )
```

time: 697 us -> 188 us (0.27)
  blocking collectives: 560 us -> 7.69 us
  Pallas kernels: 0 us -> 173 us
  waiting for transfers between devices: 68.6 us -> 0 us
  starting transfers between devices: 35.5 us -> 0 us
  local copies, waits for them, and re-layouts: 21.3 us -> 4.28 us
    psum x4 -> x0, blocking collectives: 309 us -> none  [the longest x1 287 us: body(): sample_total = lax.psum(jnp.sum(counts, axis=1), 'cls')]
    all_to_all x4 -> x0, blocking collectives: 251 us -> none  [the longest x2 126 us: body(): lax.all_to_all(outgoing.reshape(owner_count, capacity, samples_dev, TILE)...]
    pallas_call x0 -> x1, Pallas kernels: none -> 173 us  [body(): pl.pallas_call(em_kernel, out_shape=jax.ShapeDtypeStruct(start.shape, f32...]
    all_to_all x3 -> x0, waiting for transfers between devices: 68.6 us -> none  [the longest x1 54.4 us: body(): lax.all_to_all(outgoing.reshape(owner_count, capacity, samples_dev, TILE)...]
    all_to_all x3 -> x0, starting transfers between devices: 35.5 us -> none  [the longest x1 20.4 us: body(): lax.all_to_all(request.reshape(owner_count, capacity), 'cls', split_axis=...]
    unnamed x0 -> x1, blocking collectives: none -> 7.69 us
  transfers between devices with their start and end apart: 3 -> 0, of which waited for: 2 -> 0; matrix products, arithmetic and copies ran while one was open for 0% -> 0% of each run, Pallas kernels for 0% -> 0%
where the time goes in v1:
time: 188 us; the launch traced here: 187 us
  Pallas kernels  173 us (92%)
  blocking collectives  7.69 us (4%)
  local copies, waits for them, and re-layouts  4.28 us (2%)
    pallas_call x1, Pallas kernels, body(): pl.pallas_call(em_kernel, out_shape=jax.ShapeDtypeStruct(start.shape, f32...  173 us
    unnamed x1, blocking collectives  7.69 us
    unnamed x10, local copies, waits for them, and re-layouts  4.12 us

profile of v1, /device:TPU:1, one launch (start us, length us, event | category | flops | bytes accessed | tf_op | source)
XLA Modules:
  0.0 186.5 jit_solution(10362209211195589482)
XLA Ops:
  0.0 0.0 copy-start.1
  0.0 1.3 dynamic-slice
  1.9 0.7 multiply_add_fusion
  2.7 0.1 copy.8
  2.7 0.1 reshape.7
  2.8 0.2 dynamic-update-slice
  3.0 7.7 %all-reduce.tid = s32[128]{0:T(128)S(1)} all-reduce(s32[128]{0:T(128)S(1)} %dynamic-update-slice), channel_id=1, replica_groups={{0,128,256,384},{4,132,260,388},{8,136,264,392},{12,140,268,396},{16,14..., use_global_device_ids=true, to_apply=%add | all-reduce | flops 128 | bytes 1024
  10.7 0.1 fusion.2
  10.9 0.2 convert_reduce_fusion.1
  11.0 0.2 convert_reduce_fusion
  11.2 0.1 slice_compare_fusion
  11.3 0.1 add_convert_fusion.keep
  11.4 0.0 copy-done.1
  11.4 0.0 copy-start
  11.4 1.2 copy-done
  12.6 0.0 copy-start.2
  12.6 0.8 copy-done.2
  13.3 172.6 %em_rounds.1 = f32[16,512]{1,0:T(8,128)S(1)} custom-call(s32[128]{0:T(128)S(1)} %all-reduce.tid, s32[128]{0:T(128)S(1)} %get-tuple-element.7.perm, s32[128]{0:T(128)S(1)} %add_convert_fusion.keep, s32[128]{0:T(128)S(1)} %add_select_fusion.pos, f32[16,1024]{1,0:T(8,128)S(1)} %copy-done.1, bf16[8,4,128,128]{3,2,1,0:T(8,128)(2,1)S(1)} %copy-done, ...), custom_call_target="tpu_custom_call" | custom-call | tf_op jit(solution)/shard_map/em_rounds/pallas_call | solution.py:377
  185.9 0.6 copy.11
  (3 shorter events, 0.0 us)
Async XLA Ops:
  0.0 11.4 %copy-start.1 = (f32[16,1024]{1,0:T(8,128)S(1)}, f32[16,1024]{1,0:T(8,128)}, u32[]{:S(2)}) copy-start(f32[16,1024]{1,0:T(8,128)} %counts.1) | copy-start | bytes 196612
  11.4 1.2 copy-start
  12.6 0.8 copy-start.2

commit v2 on v1

--- a/solution.py
+++ b/solution.py
@@ -14,6 +14,7 @@
 MESH = pl.DeviceIdType.MESH
 NX, NZ, NC, NY = 4, 16, 2, 4
 TD = 4
+CT = 8
 LINKS = 32
 COL = NZ * NC * TD
 HALF = NZ * TD
@@ -22,11 +23,13 @@
 
 
 def em_kernel(
-    tid, perm, keep, pos, counts, compat, start, out,
-    th, xs, xr, sr, cum, d, cr, nr, sf, fr, tt, tx, tot, ps, theta,
+    owner_hbm, local_hbm, counts_hbm, compat_hbm, start_hbm, out,
+    owner, local, counts, cb, tab, raw, lists, table, th, xs, xr, sr, cum, d, cr, nr, sf, fr, tt, tx, tot, ps, theta,
     fz_s, fz_r, fc_s, fc_r, fx_s, fx_r, rx_s, rx_r, rc_s, rc_r,
-    rn_s, rn_r, rf_s, rf_r, tz_s, tz_r, tg_s, tg_r, p_s, p_r,
+    rn_s, rn_r, rf_s, rf_r, tz_s, tz_r, tg_s, tg_r, p_s, p_r, l_s, l_r, in_s,
+    pe, pr, rt, ex_s, ex_r, ey_s, ey_r, pe_s, pe_r, q_s, q_r,
 ):
+    tid, perm, keep, pos, mytile = (table.at[i] for i in range(5))
     me = lax.axis_index("cls")
     y = lax.axis_index("smp")
     c = me % NC
@@ -55,7 +58,66 @@
     barrier = pltpu.get_barrier_semaphore()
     for peer in peers:
         pl.semaphore_signal(barrier, inc=1, device_id=at(**peer), device_id_type=MESH)
+    loads = [
+        pltpu.make_async_copy(a, b, in_s.at[i])
+        for i, (a, b) in enumerate(
+            (
+                (start_hbm, theta),
+                (counts_hbm, counts),
+                (compat_hbm, cb.at[pl.ds(x * LINKS, LINKS)]),
+                (owner_hbm, owner),
+                (local_hbm, local),
+            )
+        )
+    ]
+    for load in loads:
+        load.start()
+    lane = lax.broadcasted_iota(jnp.int32, (8, TILE), 1)
+    raw[...] = jnp.zeros((8, TILE), jnp.int32)
+    loads[3].wait()
+    loads[4].wait()
+    raw[0:K, 0:CT] = owner[...] * TD + local[...]
+    row = raw[0:1, :]
+    for k in range(1, K):
+        row = row + pltpu.roll(raw[k : k + 1, :], k * CT, 1)
+    for j in (1, 2):
+        row = row + pltpu.roll(row, j * LINKS, 1)
+    tab[0] = jnp.where(lane // LINKS == x, jnp.broadcast_to(row, (8, TILE)), 0)
     pl.semaphore_wait(barrier, len(peers))
+
+    def lcopy(dx):
+        return copy(tab.at[0], tab.at[dx], l_s.at[dx - 1], l_r.at[dx - 1], at(dx=dx))
+
+    for dx in (2, 1, 3):
+        lcopy(dx).start()
+
+    def make_lists():
+        for dx in (1, 3, 2):
+            lcopy(dx).wait_recv()
+        whole = tab[0, 0:1] + tab[1, 0:1] + tab[2, 0:1] + tab[3, 0:1]
+        key = jnp.where(whole // COL == x, whole % COL, COL)
+        keys = jnp.broadcast_to(key, (TILE, TILE))
+        mine = jnp.transpose(keys)
+        j = lax.broadcasted_iota(jnp.int32, (TILE, TILE), 0)
+        i = lax.broadcasted_iota(jnp.int32, (TILE, TILE), 1)
+        before = jnp.where(keys < mine, 1, 0) + jnp.where((keys == mine) & (i < j), 1, 0)
+        rank = jnp.sum(before, axis=1, keepdims=True)
+        place = rank == i
+        order = jnp.sum(jnp.where(place, j, 0), axis=0, keepdims=True)
+        ranked = jnp.sum(jnp.where(place, mine, 0), axis=0, keepdims=True)
+        again = (ranked == pltpu.roll(ranked, 1, 1)) & (lane[0:1] > 0)
+        upto = jnp.sum(jnp.where(mine <= i, 1, 0), axis=0, keepdims=True)
+        some = jnp.sum(jnp.where(mine == i, 1, 0), axis=0, keepdims=True)
+        lists[0:1, :] = whole
+        lists[1:2, :] = order
+        lists[2:3, :] = jnp.where(again, 1, 0)
+        lists[3:4, :] = jnp.where(some > 0, upto - 1, COL)
+        lists[4:5, :] = key
+        load = pltpu.make_async_copy(lists, table, in_s.at[5])
+        load.start()
+        load.wait()
+        for dx in (1, 2, 3):
+            lcopy(dx).wait_send()
 
     far = [(0, 0, STEP), (1, 0, -STEP)]
     near_own = [(2 + j, 0, o) for j, o in enumerate(NEAR)]
@@ -114,8 +176,10 @@
         lambda zz: tt.at[zz], tz_s, tz_r, lambda k, off: None
     )
 
-    theta[...] = start[...]
+    lists[...] = jnp.zeros((8, TILE), jnp.int32)
+    loads[0].wait()
     cum[COL] = jnp.zeros((16, TILE), jnp.float32)
+    th[COL] = jnp.zeros((16, TILE), jnp.bfloat16)
 
     def total_own():
         s = counts[:, 0:TILE]
@@ -126,6 +190,17 @@
     def tg(j, dx, dc):
         return copy(tx.at[0], tx.at[1 + j], tg_s.at[j], tg_r.at[j], at(dx=dx, dc=dc))
 
+    part = LINKS // NY
+
+    def ex(dx, src_x):
+        ref = cb.at[pl.ds(src_x * LINKS + y * part, part)]
+        return copy(ref, ref, ex_s.at[dx - 1], ex_r.at[dx - 1], at(dx=dx))
+
+    def ey(dx, dy, src_y):
+        ref = cb.at[pl.ds(((x + NX - dx) % NX) * LINKS + src_y * part, part)]
+        j = (dx - 1) * 3 + dy - 1
+        return copy(ref, ref, ey_s.at[j], ey_r.at[j], at(dy=dy))
+
     def sweep(r, carry):
         for t in range(TD):
             th[(z * NC + c) * TD + t] = theta[:, t * TILE : (t + 1) * TILE].astype(jnp.bfloat16)
@@ -133,8 +208,13 @@
 
         @pl.when(r == 0)
         def _():
+            loads[1].wait()
             total_own()
             t_first()
+            loads[2].wait()
+            for dx in (2, 1, 3):
+                ex(dx, x).start()
+            make_lists()
 
         f_second()
 
@@ -155,24 +235,28 @@
                 at(dx=dx),
             )
 
-        for dx in (2, 1, 3):
-            row = ((x + dx) % NX) * LINKS
-
-            def pick(l, _, dx=dx, row=row):
-                xs[(dx - 1) * LINKS + l] = th[tid[row + l] % COL]
+        def th_sent():
+            f_close()
+            for k, off in core_steps:
+                to_core(k, off).wait_send()
+
+        def by_tiles():
+            for dx in (2, 1, 3):
+                row = ((x + dx) % NX) * LINKS
+
+                def pick(l, _, dx=dx, row=row):
+                    xs[(dx - 1) * LINKS + l] = th[tid[row + l] % COL]
+                    return 0
+
+                lax.fori_loop(0, LINKS, pick, 0, unroll=8)
+                xcopy(dx).start()
+
+            def pick_own(l, _):
+                xr[x * LINKS + l] = th[tid[x * LINKS + l] % COL]
                 return 0
 
-            lax.fori_loop(0, LINKS, pick, 0, unroll=8)
-            xcopy(dx).start()
-
-        def pick_own(l, _):
-            xr[x * LINKS + l] = th[tid[x * LINKS + l] % COL]
-            return 0
-
-        lax.fori_loop(0, LINKS, pick_own, 0, unroll=8)
-
-        @pl.when(r == 0)
-        def _():
+            lax.fori_loop(0, LINKS, pick_own, 0, unroll=8)
+
             t_third()
             s = tt[0]
             for i in range(1, NZ):
@@ -180,45 +264,126 @@
             tx[0] = s
             for j, (dx, dc) in enumerate(group):
                 tg(j, dx, dc).start()
-
-        def xwait(dx):
-            ref = xr.at[pl.ds(((x + NX - dx) % NX) * LINKS, LINKS)]
-            copy(ref, ref, fx_s.at[dx - 1], fx_r.at[dx - 1], at(dx=dx)).wait_recv()
-
-        for dx in (1, 3, 2):
-            xwait(dx)
-
-        def tile(i, _):
-            acc = jnp.zeros((16, TILE), jnp.float32)
-            for k in range(K):
-                l = i * K + k
-                got = xr[(tid[x * LINKS + l] // COL) * LINKS + l]
-                acc = acc + lax.dot_general(
-                    got, compat[i, k], (((1,), (1,)), ((), ())),
-                    preferred_element_type=jnp.float32,
+            for dx in (1, 3, 2):
+                ex(dx, (x + NX - dx) % NX).wait_recv()
+                for dy in (2, 1, 3):
+                    ey(dx, dy, y).start()
+
+            def xwait(dx):
+                ref = xr.at[pl.ds(((x + NX - dx) % NX) * LINKS, LINKS)]
+                copy(ref, ref, fx_s.at[dx - 1], fx_r.at[dx - 1], at(dx=dx)).wait_recv()
+
+            for dx in (1, 3, 2):
+                xwait(dx)
+
+            def tile(i, _):
+                acc = jnp.zeros((16, TILE), jnp.float32)
+                for k in range(K):
+                    l = k * CT + i
+                    got = xr[(tid[x * LINKS + l] // COL) * LINKS + l]
+                    acc = acc + lax.dot_general(
+                        got, cb[x * LINKS + i * K + k], (((1,), (1,)), ((), ())),
+                        preferred_element_type=jnp.float32,
+                    )
+                ratio = (counts[:, pl.ds(pl.multiple_of(i * TILE, TILE), TILE)] / acc).astype(
+                    jnp.bfloat16
                 )
-            ratio = (counts[:, pl.ds(pl.multiple_of(i * TILE, TILE), TILE)] / acc).astype(
-                jnp.bfloat16
+                for k in range(K):
+                    sr[x * LINKS + k * CT + i] = jnp.dot(
+                        ratio, cb[x * LINKS + i * K + k], preferred_element_type=jnp.float32
+                    ).astype(jnp.bfloat16)
+                return 0
+
+            lax.fori_loop(0, LINKS // K, tile, 0, unroll=2)
+
+            def scopy(dx, src_x):
+                ref = sr.at[pl.ds(src_x * LINKS, LINKS)]
+                return copy(ref, ref, rx_s.at[dx - 1], rx_r.at[dx - 1], at(dx=dx))
+
+            for dx in (2, 1, 3):
+                scopy(dx, x).start()
+            th_sent()
+            for dx in (1, 3, 2):
+                scopy(dx, (x + NX - dx) % NX).wait_recv()
+            for dx in (1, 2, 3):
+                xcopy(dx).wait_send()
+                scopy(dx, x).wait_send()
+                ex(dx, x).wait_send()
+
+
+        def pcopy_x(dx):
+            return copy(
+                pe.at[pl.ds(dx * CT, CT)], pr.at[pl.ds((dx - 1) * CT, CT)],
+                pe_s.at[dx - 1], pe_r.at[dx - 1], at(dx=dx),
             )
-            for k in range(K):
-                sr[x * LINKS + i * K + k] = jnp.dot(
-                    ratio, compat[i, k], preferred_element_type=jnp.float32
+
+        def qcopy(dx, src_x):
+            ref = rt.at[pl.ds(src_x * CT, CT)]
+            return copy(ref, ref, q_s.at[dx - 1], q_r.at[dx - 1], at(dx=dx))
+
+        def by_sums():
+            @pl.when(r == 1)
+            def _():
+                for dx in (1, 2, 3):
+                    for dy in (1, 2, 3):
+                        ey(dx, dy, (y + NY - dy) % NY).wait_recv()
+
+            for dx in (2, 1, 3, 0):
+                row = ((x + dx) % NX) * LINKS
+
+                def part_sum(i, _, dx=dx, row=row):
+                    acc = jnp.zeros((16, TILE), jnp.float32)
+                    for k in range(K):
+                        acc = acc + lax.dot_general(
+                            th[mytile[row + k * CT + i]], cb[row + i * K + k],
+                            (((1,), (1,)), ((), ())), preferred_element_type=jnp.float32,
+                        )
+                    pe[dx * CT + i] = acc
+                    return 0
+
+                lax.fori_loop(0, CT, part_sum, 0, unroll=4)
+                if dx:
+                    pcopy_x(dx).start()
+            th_sent()
+            for dx in (1, 3, 2):
+                pcopy_x(dx).wait_recv()
+
+            def ratio(i, _):
+                acc = pe[i] + pr[i] + pr[CT + i] + pr[2 * CT + i]
+                rt[x * CT + i] = (
+                    counts[:, pl.ds(pl.multiple_of(i * TILE, TILE), TILE)] / acc
                 ).astype(jnp.bfloat16)
-            return 0
-
-        lax.fori_loop(0, LINKS // K, tile, 0, unroll=2)
-
-        def scopy(dx, src_x):
-            ref = sr.at[pl.ds(src_x * LINKS, LINKS)]
-            return copy(ref, ref, rx_s.at[dx - 1], rx_r.at[dx - 1], at(dx=dx))
-
-        for dx in (2, 1, 3):
-            scopy(dx, x).start()
-        f_close()
-        for k, off in core_steps:
-            to_core(k, off).wait_send()
-        for dx in (1, 3, 2):
-            scopy(dx, (x + NX - dx) % NX).wait_recv()
+                return 0
+
+            lax.fori_loop(0, CT, ratio, 0, unroll=4)
+            for dx in (2, 1, 3):
+                qcopy(dx, x).start()
+            for dx in (0, 1, 3, 2):
+                src_x = (x + NX - dx) % NX
+                if dx:
+                    qcopy(dx, src_x).wait_recv()
+
+                def shares(i, _, src_x=src_x):
+                    for k in range(K):
+                        sr[src_x * LINKS + k * CT + i] = jnp.dot(
+                            rt[src_x * CT + i], cb[src_x * LINKS + i * K + k],
+                            preferred_element_type=jnp.float32,
+                        ).astype(jnp.bfloat16)
+                    return 0
+
+                lax.fori_loop(0, CT, shares, 0, unroll=4)
+            for dx in (1, 2, 3):
+                pcopy_x(dx).wait_send()
+                qcopy(dx, x).wait_send()
+
+            @pl.when(r == 1)
+            def _():
+                for dx in (1, 2, 3):
+                    for dy in (1, 2, 3):
+                        ey(dx, dy, y).wait_send()
+
+        pl.when(r == 0)(by_tiles)
+        pl.when(r > 0)(by_sums)
 
         def add(j, acc):
             acc = jnp.where(keep[j] > 0, acc, 0.0) + sr[perm[j]].astype(jnp.float32)
@@ -319,9 +484,6 @@
 
         for dy in (2, 1, 3):
             pcopy(dy).start()
-        for dx in (1, 2, 3):
-            xcopy(dx).wait_send()
-            scopy(dx, x).wait_send()
         rcopy.wait_send()
         for n in nsteps:
             ncopy(*n).wait_send()
@@ -347,26 +509,7 @@
 
 
 def body(counts, compat, link_owner, link_local, start):
-    x = lax.axis_index("cls") // (NZ * NC)
-    mine = (link_owner * TD + link_local).reshape(-1)
-    groups = [[(i * NZ + j) * NC + k for i in range(NX)] for j in range(NZ) for k in range(NC)]
-    tid = lax.all_gather(mine, "cls", axis_index_groups=groups, tiled=True)
-    key = jnp.where(tid // COL == x, tid % COL, COL)
-    order = jnp.arange(COL, dtype=jnp.int32)
-    before = (key[None, :] < key[:, None]) | (
-        (key[None, :] == key[:, None]) & (order[None, :] < order[:, None])
-    )
-    rank = jnp.sum(before.astype(jnp.int32), axis=1)
-    place = rank[None, :] == order[:, None]
-    perm = jnp.sum(jnp.where(place, order[None, :], 0), axis=1)
-    skey = jnp.sum(jnp.where(place, key[None, :], 0), axis=1)
-    keep = jnp.concatenate(
-        [jnp.zeros((1,), jnp.int32), (skey[1:] == skey[:-1]).astype(jnp.int32)]
-    )
-    upto = jnp.sum((key[None, :] <= order[:, None]).astype(jnp.int32), axis=1)
-    some = jnp.any(key[None, :] == order[:, None], axis=1)
-    pos = jnp.where(some, upto - 1, COL)
-    smem = pl.BlockSpec(memory_space=pltpu.SMEM)
+    hbm = pl.BlockSpec(memory_space=pltpu.HBM)
     vmem = pl.BlockSpec(memory_space=pltpu.VMEM)
     f32, bf16 = jnp.float32, jnp.bfloat16
     dma = pltpu.SemaphoreType.DMA
@@ -377,10 +520,18 @@
     return pl.pallas_call(
         em_kernel,
         out_shape=jax.ShapeDtypeStruct(start.shape, f32),
-        in_specs=[smem] * 4 + [vmem] * 3,
+        in_specs=[hbm] * 5,
         out_specs=vmem,
         scratch_shapes=[
-            buf(COL, bf16),
+            pltpu.VMEM((K, CT), jnp.int32),
+            pltpu.VMEM((K, CT), jnp.int32),
+            pltpu.VMEM(counts.shape, f32),
+            pltpu.VMEM((NX * LINKS, TILE, TILE), bf16),
+            pltpu.VMEM((NX, 8, TILE), jnp.int32),
+            pltpu.VMEM((8, TILE), jnp.int32),
+            pltpu.VMEM((8, TILE), jnp.int32),
+            pltpu.SMEM((8, TILE), jnp.int32),
+            buf(COL + 1, bf16),
             buf(3 * LINKS, bf16),
             buf(NX * LINKS, bf16),
             buf(NX * LINKS, bf16),
@@ -405,12 +556,20 @@
             dma((15,)), dma((15,)),
             dma((7,)), dma((7,)),
             dma((9,)), dma((9,)),
+            dma((3,)), dma((3,)), dma((6,)),
+            buf(NX * CT, f32),
+            buf(3 * CT, f32),
+            buf(NX * CT, bf16),
+            dma((3,)), dma((3,)),
+            dma((9,)), dma((9,)),
+            dma((3,)), dma((3,)),
+            dma((3,)), dma((3,)),
         ],
         compiler_params=pltpu.CompilerParams(
-            collective_id=0, has_side_effects=True, vmem_limit_bytes=40 << 20
+            collective_id=0, has_side_effects=True, vmem_limit_bytes=60 << 20
         ),
         name="em_rounds",
-    )(tid, perm, keep, pos, counts, compat, start)
+    )(link_owner.T, link_local.T, counts, compat.reshape(LINKS, TILE, TILE), start)
 
 
 def solution(mesh):

time: 188 us -> 164 us (0.87)
  Pallas kernels: 173 us -> 161 us
  blocking collectives: 7.69 us -> 0 us
  local copies, waits for them, and re-layouts: 4.28 us -> 1.38 us
    pallas_call x1, Pallas kernels: 173 us -> 161 us  [body(): pl.pallas_call(em_kernel, out_shape=jax.ShapeDtypeStruct(start.shape, f32...]
    unnamed x1 -> x0, blocking collectives: 7.69 us -> none
    unnamed x10 -> x1, local copies, waits for them, and re-layouts: 4.12 us -> 1.38 us
where the time goes in v2:
time: 164 us; the launch traced here: 163 us
  Pallas kernels  161 us (98%)
    pallas_call x1, Pallas kernels, body(): pl.pallas_call(em_kernel, out_shape=jax.ShapeDtypeStruct(start.shape, f32...  161 us

profile of v2, /device:TPU:1, one launch (start us, length us, event | category | flops | bytes accessed | tf_op | source)
XLA Modules:
  0.0 162.7 jit_solution(5844721755557243950)
XLA Ops:
  0.0 161.3 %em_rounds.1 = f32[16,512]{1,0:T(8,128)} custom-call(s32[4,8]{1,0:T(4,128)} %bitcast.4, s32[4,8]{1,0:T(4,128)} %bitcast.5, f32[16,1024]{1,0:T(8,128)} %counts_hbm.1, bf16[32,128,128]{2,1,0:T(8,128)(2,1)} %bitcast.3, f32[16,512]{1,0:T(8,128)} %start_hbm.1), custom_call_target="tpu_custom_call" | custom-call | tf_op jit(solution)/shard_map/em_rounds/pallas_call | solution.py:520
  161.3 1.4 copy.7

commit v3 on v2

--- a/solution.py
+++ b/solution.py
@@ -27,7 +27,7 @@
     owner, local, counts, cb, tab, raw, lists, table, th, xs, xr, sr, cum, d, cr, nr, sf, fr, tt, tx, tot, ps, theta,
     fz_s, fz_r, fc_s, fc_r, fx_s, fx_r, rx_s, rx_r, rc_s, rc_r,
     rn_s, rn_r, rf_s, rf_r, tz_s, tz_r, tg_s, tg_r, p_s, p_r, l_s, l_r, in_s,
-    pe, pr, rt, ex_s, ex_r, ey_s, ey_r, pe_s, pe_r, q_s, q_r,
+    tf, tf_s, tf_r, pq, rows, sums, pe, pr, rt, ex_s, ex_r, ey_s, ey_r, pe_s, pe_r, q_s, q_r,
 ):
     tid, perm, keep, pos, mytile = (table.at[i] for i in range(5))
     me = lax.axis_index("cls")
@@ -36,8 +36,10 @@
     z = (me // NC) % NZ
     x = me // (NC * NZ)
 
+    turn = 1 - 2 * c
+
     def zrel(off):
-        return (z + off + NZ) % NZ
+        return (z + turn * off + NZ) % NZ
 
     def at(dx=0, dz=0, dc=0, dy=0):
         return (
@@ -55,6 +57,7 @@
     peers += [dict(dc=1)] + [dict(dx=o) for o in (1, 2, 3)] + [dict(dy=o) for o in (1, 2, 3)]
     group = [(dx, dc) for dx in range(NX) for dc in range(NC) if (dx, dc) != (0, 0)]
     peers += [dict(dx=dx, dc=1) for dx in (1, 2, 3)]
+    peers += [dict(dz=o, dy=dy) for o in (STEP, -STEP) for dy in (1, 2, 3)]
     barrier = pltpu.get_barrier_semaphore()
     for peer in peers:
         pl.semaphore_signal(barrier, inc=1, device_id=at(**peer), device_id_type=MESH)
@@ -165,7 +168,7 @@
         return ref
 
     def to_core(k, off, mine=True):
-        ref = th_blk(c if mine else 1 - c)(zrel(off))
+        ref = th_blk(c if mine else 1 - c)(zrel(off if mine else -off))
         return copy(ref, ref, fc_s.at[k], fc_r.at[k], at(dc=1))
 
     f_first, f_second, f_third, f_close = spread(
@@ -223,6 +226,14 @@
             t_second()
 
         f_third()
+
+        def tcopy(j, way):
+            k = r * 2 + j
+            return copy(theta, tf.at[k], tf_s.at[k], tf_r.at[k], at(dz=way))
+
+        relays = ((0, STEP), (1, -STEP))
+        for j, way in relays:
+            tcopy(j, way).start()
         for k, off in core_steps:
             to_core(k, off, mine=False).wait_recv()
 
@@ -441,7 +452,30 @@
         ]
         for n in order:
             ncopy(*n).start()
-        for j, kind in ((0, STEP), (1, -STEP)):
+
+        @pl.when(r == 0)
+        def _():
+            for j, (dx, dc) in enumerate(group):
+                tg(j, dx, dc).wait_recv()
+            s = tx[0]
+            for j in range(len(group)):
+                s = s + tx[1 + j]
+            tot[...] = jnp.broadcast_to(jnp.sum(s, axis=1, keepdims=True), (16, TILE))
+
+        def pcopy(kind, way, dy):
+            j = (r * 3 + kind) * 3 + dy - 1
+            return copy(ps.at[r * 3 + kind], pq.at[j], p_s.at[j], p_r.at[j], at(dz=way, dy=dy))
+
+        def pool(kind, way, weight, sums):
+            for t in range(TD):
+                cols = slice(t * TILE, (t + 1) * TILE)
+                part = weight(cols) * sums(t) / tot[...]
+                ps[r * 3 + kind, :, cols] = jnp.sum(part, axis=0, keepdims=True)
+            for dy in (2, 1, 3):
+                pcopy(kind, way, dy).start()
+
+        ways = ((0, 0), (1, STEP), (2, -STEP))
+        for j, kind in relays:
             slots = [jj * 3 + 1 + j for jj in range(4)] + ([12] if j == 0 else [])
             for n in nsteps:
                 if n[0] in slots:
@@ -452,38 +486,33 @@
                     acc = acc + nr[s * TD + t]
                 sf[j * TD + t] = acc
             fcopy(j, kind).start()
+        for j, kind in relays:
+            tcopy(1 - j, kind).wait_recv()
+            pool(
+                1 + j, kind, lambda cols, j=j: tf[r * 2 + 1 - j, :, cols],
+                lambda t, j=j: sf[j * TD + t],
+            )
         own = [jj * 3 for jj in range(4)]
         for n in nsteps:
             if n[0] in own:
                 ncopy(*n).wait_recv()
 
-        @pl.when(r == 0)
-        def _():
-            for j, (dx, dc) in enumerate(group):
-                tg(j, dx, dc).wait_recv()
-            s = tx[0]
-            for j in range(len(group)):
-                s = s + tx[1 + j]
-            tot[...] = jnp.broadcast_to(jnp.sum(s, axis=1, keepdims=True), (16, TILE))
-
+        for t in range(TD):
+            acc = d[c * HALF + z * TD + t]
+            for i in own:
+                acc = acc + nr[i * TD + t]
+            sums[t] = acc
+        pool(0, 0, lambda cols: theta[:, cols], lambda t: sums[t])
+        for j, kind in relays:
+            tcopy(j, kind).wait_send()
         fcopy(0, STEP).wait_recv()
         fcopy(1, -STEP).wait_recv()
         for t in range(TD):
-            acc = d[c * HALF + z * TD + t]
-            for s in own:
-                acc = acc + nr[s * TD + t]
-            acc = acc + (fr[t] + fr[TD + t])
             cols = slice(t * TILE, (t + 1) * TILE)
-            updated = theta[:, cols] * acc / tot[...]
+            updated = theta[:, cols] * (sums[t] + (fr[t] + fr[TD + t])) / tot[...]
             theta[:, cols] = updated
-            ps[r * NY, :, cols] = jnp.sum(updated, axis=0, keepdims=True)
-
-        def pcopy(dy):
-            return copy(ps.at[r * NY], ps.at[r * NY + dy], p_s.at[r * 3 + dy - 1],
-                        p_r.at[r * 3 + dy - 1], at(dy=dy))
-
-        for dy in (2, 1, 3):
-            pcopy(dy).start()
+            rows[:, cols] = jnp.sum(updated, axis=0, keepdims=True)
+
         rcopy.wait_send()
         for n in nsteps:
             ncopy(*n).wait_send()
@@ -496,12 +525,15 @@
             for j, (dx, dc) in enumerate(group):
                 tg(j, dx, dc).wait_send()
 
-        for dy in (1, 3, 2):
-            pcopy(dy).wait_recv()
-        pooled = ps[r * NY] + ps[r * NY + 1] + ps[r * NY + 2] + ps[r * NY + 3]
+        pooled = rows[...]
+        for kind, way in ways:
+            for dy in (1, 3, 2):
+                pcopy(kind, way, dy).wait_recv()
+                pooled = pooled + pq[(r * 3 + kind) * 3 + dy - 1]
         theta[...] = (1.0 - MIXING) * theta[...] + (MIXING / (16 * NY)) * pooled
-        for dy in (1, 2, 3):
-            pcopy(dy).wait_send()
+        for kind, way in ways:
+            for dy in (1, 2, 3):
+                pcopy(kind, way, dy).wait_send()
         return carry
 
     lax.fori_loop(0, ITERS, sweep, 0)
@@ -544,7 +576,7 @@
             buf(NZ, f32),
             buf(NX * NC, f32),
             pltpu.VMEM((16, TILE), f32),
-            pltpu.VMEM((ITERS * NY, 1, TD * TILE), f32),
+            pltpu.VMEM((ITERS * 3, 1, TD * TILE), f32),
             pltpu.VMEM((16, TD * TILE), f32),
             dma((15,)), dma((15,)),
             dma((16,)), dma((16,)),
@@ -555,8 +587,13 @@
             dma((2,)), dma((2,)),
             dma((15,)), dma((15,)),
             dma((7,)), dma((7,)),
-            dma((9,)), dma((9,)),
+            dma((ITERS * 9,)), dma((ITERS * 9,)),
             dma((3,)), dma((3,)), dma((6,)),
+            pltpu.VMEM((ITERS * 2, 16, TD * TILE), f32),
+            dma((ITERS * 2,)), dma((ITERS * 2,)),
+            pltpu.VMEM((ITERS * 9, 1, TD * TILE), f32),
+            pltpu.VMEM((1, TD * TILE), f32),
+            buf(TD, f32),
             buf(NX * CT, f32),
             buf(3 * CT, f32),
             buf(NX * CT, bf16),

time: 164 us -> 162 us (0.988)
  no operation moved by 1% of the time
where the time goes in v3:
time: 162 us
  Pallas kernels  161 us (99%)
    pallas_call x1, Pallas kernels, body(): pl.pallas_call(em_kernel, out_shape=jax.ShapeDtypeStruct(start.shape, f32...  161 us

profile of v3, /device:TPU:1, one launch (start us, length us, event | category | flops | bytes accessed | tf_op | source)
XLA Modules:
  0.0 162.1 jit_solution(18282635050005148667)
XLA Ops:
  0.0 160.8 %em_rounds.1 = f32[16,512]{1,0:T(8,128)} custom-call(s32[4,8]{1,0:T(4,128)} %bitcast.4, s32[4,8]{1,0:T(4,128)} %bitcast.5, f32[16,1024]{1,0:T(8,128)} %counts_hbm.1, bf16[32,128,128]{2,1,0:T(8,128)(2,1)} %bitcast.3, f32[16,512]{1,0:T(8,128)} %start_hbm.1), custom_call_target="tpu_custom_call" | custom-call | tf_op jit(solution)/shard_map/em_rounds/pallas_call | solution.py:552
  160.8 1.4 copy.7

commit v4 on v2

--- a/solution.py
+++ b/solution.py
@@ -18,8 +18,8 @@
 LINKS = 32
 COL = NZ * NC * TD
 HALF = NZ * TD
-STEP = 5
-NEAR = (1, -1, 2, -2)
+FAR = (6, -6, 3, -3)
+NEAR = (1, -1)
 
 
 def em_kernel(
@@ -27,23 +27,26 @@
     owner, local, counts, cb, tab, raw, lists, table, th, xs, xr, sr, cum, d, cr, nr, sf, fr, tt, tx, tot, ps, theta,
     fz_s, fz_r, fc_s, fc_r, fx_s, fx_r, rx_s, rx_r, rc_s, rc_r,
     rn_s, rn_r, rf_s, rf_r, tz_s, tz_r, tg_s, tg_r, p_s, p_r, l_s, l_r, in_s,
-    pe, pr, rt, ex_s, ex_r, ey_s, ey_r, pe_s, pe_r, q_s, q_r,
+    sums, pe, pr, rt, ex_s, ex_r, ey_s, ey_r, pe_s, pe_r, q_s, q_r,
 ):
-    tid, perm, keep, pos, mytile = (table.at[i] for i in range(5))
+    tid, perm, keep, pos, mytile, place = (table.at[i] for i in range(6))
     me = lax.axis_index("cls")
     y = lax.axis_index("smp")
     c = me % NC
     z = (me // NC) % NZ
     x = me // (NC * NZ)
 
+    turn = 1 - 2 * c
+
+    zs = {off: lax.rem(z + turn * off + NZ, NZ) for off in range(-8, 9)}
+
     def zrel(off):
-        return (z + off + NZ) % NZ
+        return zs[off]
+
+    devs = {}
 
     def at(dx=0, dz=0, dc=0, dy=0):
-        return (
-            ((((x + dx) % NX) * NZ + zrel(dz)) * NC + (c + dc) % NC),
-            (y + dy) % NY,
-        )
+        return devs[(dx, dz, dc, dy)]
 
     def copy(src, dst, send, recv, dev):
         return pltpu.make_async_remote_copy(
@@ -51,13 +54,17 @@
             device_id=dev, device_id_type=MESH,
         )
 
-    peers = [dict(dz=o) for o in (1, -1, 2, -2, 3, -3, STEP, -STEP)]
-    peers += [dict(dc=1)] + [dict(dx=o) for o in (1, 2, 3)] + [dict(dy=o) for o in (1, 2, 3)]
     group = [(dx, dc) for dx in range(NX) for dc in range(NC) if (dx, dc) != (0, 0)]
-    peers += [dict(dx=dx, dc=1) for dx in (1, 2, 3)]
+    peers = [(0, o, 0, 0) for o in (1, -1, 2, -2) + FAR] + [(0, 0, 0, dy) for dy in (1, 2, 3)]
+    peers += [(dx, 0, dc, 0) for dx, dc in group]
+    for dx, dz, dc, dy in peers:
+        devs[(dx, dz, dc, dy)] = (
+            (lax.rem(x + dx, NX) * NZ + zs[dz]) * NC + lax.rem(c + dc, NC),
+            lax.rem(y + dy, NY),
+        )
     barrier = pltpu.get_barrier_semaphore()
     for peer in peers:
-        pl.semaphore_signal(barrier, inc=1, device_id=at(**peer), device_id_type=MESH)
+        pl.semaphore_signal(barrier, inc=1, device_id=at(*peer), device_id_type=MESH)
     loads = [
         pltpu.make_async_copy(a, b, in_s.at[i])
         for i, (a, b) in enumerate(
@@ -102,9 +109,9 @@
         i = lax.broadcasted_iota(jnp.int32, (TILE, TILE), 1)
         before = jnp.where(keys < mine, 1, 0) + jnp.where((keys == mine) & (i < j), 1, 0)
         rank = jnp.sum(before, axis=1, keepdims=True)
-        place = rank == i
-        order = jnp.sum(jnp.where(place, j, 0), axis=0, keepdims=True)
-        ranked = jnp.sum(jnp.where(place, mine, 0), axis=0, keepdims=True)
+        at_rank = rank == i
+        order = jnp.sum(jnp.where(at_rank, j, 0), axis=0, keepdims=True)
+        ranked = jnp.sum(jnp.where(at_rank, mine, 0), axis=0, keepdims=True)
         again = (ranked == pltpu.roll(ranked, 1, 1)) & (lane[0:1] > 0)
         upto = jnp.sum(jnp.where(mine <= i, 1, 0), axis=0, keepdims=True)
         some = jnp.sum(jnp.where(mine == i, 1, 0), axis=0, keepdims=True)
@@ -112,20 +119,23 @@
         lists[1:2, :] = order
         lists[2:3, :] = jnp.where(again, 1, 0)
         lists[3:4, :] = jnp.where(some > 0, upto - 1, COL)
-        lists[4:5, :] = key
+        col = whole % COL
+        lies = (col // TD) % NC * HALF + col // (TD * NC) * TD + col % TD
+        lists[4:5, :] = jnp.where(key < COL, lies, COL)
+        lists[5:6, :] = lies
         load = pltpu.make_async_copy(lists, table, in_s.at[5])
         load.start()
         load.wait()
         for dx in (1, 2, 3):
             lcopy(dx).wait_send()
 
-    far = [(0, 0, STEP), (1, 0, -STEP)]
-    near_own = [(2 + j, 0, o) for j, o in enumerate(NEAR)]
-    near_low = [(6 + j, -STEP, o) for j, o in enumerate(NEAR)] + [(10, -STEP, 3)]
-    near_high = [(11 + j, STEP, o) for j, o in enumerate(NEAR)]
-    every = far + near_own + near_low + near_high
-
-    def spread(blk, send, recv, arrived):
+    far = [(j, 0, o) for j, o in enumerate(FAR)]
+    near_own = [(4 + j, 0, o) for j, o in enumerate(NEAR)]
+    near_of = [[(6 + 2 * i + j, -w, o) for j, o in enumerate(NEAR)] for i, w in enumerate(FAR)]
+    near_of[0].append((14, -FAR[0], 2))
+    every = far + near_own + [step for steps in near_of for step in steps]
+
+    def spread(blk, send, recv):
         def move(k, off, way):
             ref = blk(zrel(off))
             return copy(ref, ref, send.at[k], recv.at[k], at(dz=way))
@@ -133,24 +143,21 @@
         def take(k, off, way):
             ref = blk(zrel(off - way))
             copy(ref, ref, send.at[k], recv.at[k], at(dz=way)).wait_recv()
-            arrived(1 + k, off - way)
 
         def first():
             for k, off, way in far + near_own:
                 move(k, off, way).start()
-            arrived(0, 0)
 
         def second():
-            take(*far[0])
-            for step in near_low:
-                move(*step).start()
-            take(*far[1])
-            for step in near_high:
-                move(*step).start()
+            for i in (2, 3, 0, 1):
+                take(*far[i])
+                for step in near_of[i]:
+                    move(*step).start()
 
         def third():
-            for step in near_own + near_low + near_high:
-                take(*step)
+            for steps in [near_own] + [near_of[i] for i in (2, 3, 0, 1)]:
+                for step in steps:
+                    take(*step)
 
         def close():
             for step in every:
@@ -158,23 +165,15 @@
 
         return first, second, third, close
 
-    def th_blk(core):
-        def ref(zz):
-            return th.at[pl.ds((zz * NC + core) * TD, TD)]
-
-        return ref
-
-    def to_core(k, off, mine=True):
-        ref = th_blk(c if mine else 1 - c)(zrel(off))
-        return copy(ref, ref, fc_s.at[k], fc_r.at[k], at(dc=1))
-
-    f_first, f_second, f_third, f_close = spread(
-        th_blk(c), fz_s, fz_r, lambda k, off: to_core(k, off).start()
-    )
-    core_steps = [(0, 0)] + [(1 + k, off - way) for k, off, way in every]
-    t_first, t_second, t_third, t_close = spread(
-        lambda zz: tt.at[zz], tz_s, tz_r, lambda k, off: None
-    )
+    def th_blk(zz):
+        return th.at[pl.ds(c * HALF + zz * TD, TD)]
+
+    def to_core(core):
+        ref = th.at[pl.ds(core * HALF, HALF)]
+        return copy(ref, ref, fc_s.at[0], fc_r.at[0], at(dc=1))
+
+    f_first, f_second, f_third, f_close = spread(th_blk, fz_s, fz_r)
+    t_first, t_second, t_third, t_close = spread(lambda zz: tt.at[zz], tz_s, tz_r)
 
     lists[...] = jnp.zeros((8, TILE), jnp.int32)
     loads[0].wait()
@@ -203,7 +202,7 @@
 
     def sweep(r, carry):
         for t in range(TD):
-            th[(z * NC + c) * TD + t] = theta[:, t * TILE : (t + 1) * TILE].astype(jnp.bfloat16)
+            th[c * HALF + z * TD + t] = theta[:, t * TILE : (t + 1) * TILE].astype(jnp.bfloat16)
         f_first()
 
         @pl.when(r == 0)
@@ -223,8 +222,9 @@
             t_second()
 
         f_third()
-        for k, off in core_steps:
-            to_core(k, off, mine=False).wait_recv()
+
+        to_core(c).start()
+        to_core(1 - c).wait_recv()
 
         def xcopy(dx):
             return copy(
@@ -237,22 +237,21 @@
 
         def th_sent():
             f_close()
-            for k, off in core_steps:
-                to_core(k, off).wait_send()
+            to_core(c).wait_send()
 
         def by_tiles():
             for dx in (2, 1, 3):
                 row = ((x + dx) % NX) * LINKS
 
                 def pick(l, _, dx=dx, row=row):
-                    xs[(dx - 1) * LINKS + l] = th[tid[row + l] % COL]
+                    xs[(dx - 1) * LINKS + l] = th[place[row + l]]
                     return 0
 
                 lax.fori_loop(0, LINKS, pick, 0, unroll=8)
                 xcopy(dx).start()
 
             def pick_own(l, _):
-                xr[x * LINKS + l] = th[tid[x * LINKS + l] % COL]
+                xr[x * LINKS + l] = th[place[x * LINKS + l]]
                 return 0
 
             lax.fori_loop(0, LINKS, pick_own, 0, unroll=8)
@@ -418,12 +417,12 @@
         def dz(off):
             return d.at[pl.ds(c * HALF + zrel(off) * TD, TD)]
 
-        kinds = (0, STEP, -STEP)
+        kinds = (0,) + FAR
         nsteps = [
-            (j * 3 + k, way, way + kind)
-            for j, way in enumerate(NEAR)
-            for k, kind in enumerate(kinds)
-        ] + [(12, 3, 8)]
+            [(q * 2 + j, way, way + kind) for j, way in enumerate(NEAR)]
+            for q, kind in enumerate(kinds)
+        ]
+        nsteps[1].append((10, 2, 8))
 
         def ncopy(slot, way, dest):
             return copy(
@@ -436,26 +435,9 @@
                 at(dz=way),
             )
 
-        order = [n for n in nsteps if n[0] % 3 or n[0] == 12] + [
-            n for n in nsteps if n[0] % 3 == 0 and n[0] != 12
-        ]
-        for n in order:
-            ncopy(*n).start()
-        for j, kind in ((0, STEP), (1, -STEP)):
-            slots = [jj * 3 + 1 + j for jj in range(4)] + ([12] if j == 0 else [])
-            for n in nsteps:
-                if n[0] in slots:
-                    ncopy(*n).wait_recv()
-            for t in range(TD):
-                acc = d[c * HALF + zrel(kind) * TD + t]
-                for s in slots:
-                    acc = acc + nr[s * TD + t]
-                sf[j * TD + t] = acc
-            fcopy(j, kind).start()
-        own = [jj * 3 for jj in range(4)]
-        for n in nsteps:
-            if n[0] in own:
-                ncopy(*n).wait_recv()
+        for q in (1, 2, 3, 4):
+            for n in nsteps[q]:
+                ncopy(*n).start()
 
         @pl.when(r == 0)
         def _():
@@ -466,29 +448,48 @@
                 s = s + tx[1 + j]
             tot[...] = jnp.broadcast_to(jnp.sum(s, axis=1, keepdims=True), (16, TILE))
 
-        fcopy(0, STEP).wait_recv()
-        fcopy(1, -STEP).wait_recv()
+        for q, kind in enumerate(kinds):
+            if q == 0:
+                continue
+            for n in nsteps[q]:
+                ncopy(*n).wait_recv()
+            for t in range(TD):
+                acc = d[c * HALF + zrel(kind) * TD + t]
+                for n in nsteps[q]:
+                    acc = acc + nr[n[0] * TD + t]
+                sf[(q - 1) * TD + t] = acc
+            fcopy(q - 1, kind).start()
+            if q == 2:
+                for n in nsteps[0]:
+                    ncopy(*n).start()
+        for n in nsteps[0]:
+            ncopy(*n).wait_recv()
         for t in range(TD):
             acc = d[c * HALF + z * TD + t]
-            for s in own:
-                acc = acc + nr[s * TD + t]
-            acc = acc + (fr[t] + fr[TD + t])
+            for n in nsteps[0]:
+                acc = acc + nr[n[0] * TD + t]
+            sums[t] = acc
+        for j in (2, 3, 0, 1):
+            fcopy(j, FAR[j]).wait_recv()
+        for t in range(TD):
             cols = slice(t * TILE, (t + 1) * TILE)
+            acc = sums[t] + ((fr[t] + fr[TD + t]) + (fr[2 * TD + t] + fr[3 * TD + t]))
             updated = theta[:, cols] * acc / tot[...]
             theta[:, cols] = updated
             ps[r * NY, :, cols] = jnp.sum(updated, axis=0, keepdims=True)
 
         def pcopy(dy):
-            return copy(ps.at[r * NY], ps.at[r * NY + dy], p_s.at[r * 3 + dy - 1],
-                        p_r.at[r * 3 + dy - 1], at(dy=dy))
+            j = r * 3 + dy - 1
+            return copy(ps.at[r * NY], ps.at[r * NY + dy], p_s.at[j], p_r.at[j], at(dy=dy))
 
         for dy in (2, 1, 3):
             pcopy(dy).start()
         rcopy.wait_send()
-        for n in nsteps:
-            ncopy(*n).wait_send()
-        fcopy(0, STEP).wait_send()
-        fcopy(1, -STEP).wait_send()
+        for steps in nsteps:
+            for n in steps:
+                ncopy(*n).wait_send()
+        for j, way in enumerate(FAR):
+            fcopy(j, way).wait_send()
 
         @pl.when(r == 0)
         def _():
@@ -538,25 +539,26 @@
             buf(COL + 1, f32),
             buf(COL, f32),
             buf(HALF, f32),
-            buf(13 * TD, f32),
-            buf(2 * TD, f32),
-            buf(2 * TD, f32),
+            buf(11 * TD, f32),
+            buf(4 * TD, f32),
+            buf(4 * TD, f32),
             buf(NZ, f32),
             buf(NX * NC, f32),
             pltpu.VMEM((16, TILE), f32),
             pltpu.VMEM((ITERS * NY, 1, TD * TILE), f32),
             pltpu.VMEM((16, TD * TILE), f32),
             dma((15,)), dma((15,)),
-            dma((16,)), dma((16,)),
+            dma((1,)), dma((1,)),
             dma((3,)), dma((3,)),
             dma((3,)), dma((3,)),
             dma((1,)), dma((1,)),
-            dma((13,)), dma((13,)),
-            dma((2,)), dma((2,)),
+            dma((11,)), dma((11,)),
+            dma((4,)), dma((4,)),
             dma((15,)), dma((15,)),
             dma((7,)), dma((7,)),
-            dma((9,)), dma((9,)),
+            dma((ITERS * 3,)), dma((ITERS * 3,)),
             dma((3,)), dma((3,)), dma((6,)),
+            buf(TD, f32),
             buf(NX * CT, f32),
             buf(3 * CT, f32),
             buf(NX * CT, bf16),

time: 164 us -> 156 us (0.951)
  Pallas kernels: 161 us -> 154 us
    pallas_call x1, Pallas kernels: 161 us -> 154 us  [body(): pl.pallas_call(em_kernel, out_shape=jax.ShapeDtypeStruct(start.shape, f32...]
where the time goes in v4:
time: 156 us; the launch traced here: 155 us
  Pallas kernels  154 us (99%)
    pallas_call x1, Pallas kernels, body(): pl.pallas_call(em_kernel, out_shape=jax.ShapeDtypeStruct(start.shape, f32...  154 us

profile of v4, /device:TPU:1, one launch (start us, length us, event | category | flops | bytes accessed | tf_op | source)
XLA Modules:
  0.0 155.2 jit_solution(4898098439532441336)
XLA Ops:
  0.0 153.8 %em_rounds.1 = f32[16,512]{1,0:T(8,128)} custom-call(s32[4,8]{1,0:T(4,128)} %bitcast.4, s32[4,8]{1,0:T(4,128)} %bitcast.5, f32[16,1024]{1,0:T(8,128)} %counts_hbm.1, bf16[32,128,128]{2,1,0:T(8,128)(2,1)} %bitcast.3, f32[16,512]{1,0:T(8,128)} %start_hbm.1), custom_call_target="tpu_custom_call" | custom-call | tf_op jit(solution)/shard_map/em_rounds/pallas_call | solution.py:521
  153.8 1.4 copy.7

commit v5 on v4

--- a/solution.py
+++ b/solution.py
@@ -20,6 +20,8 @@
 HALF = NZ * TD
 FAR = (6, -6, 3, -3)
 NEAR = (1, -1)
+PLACES = (5, 6, 7, 8, -7, -6, -5, 2, 3, 4, -4, -3, -2, -1, 0, 1)
+GROUPS = ((0, 4), (4, 3), (7, 3), (10, 3), (13, 3))
 
 
 def em_kernel(
@@ -97,6 +99,9 @@
 
     for dx in (2, 1, 3):
         lcopy(dx).start()
+
+    def load_lists():
+        return pltpu.make_async_copy(lists, table, in_s.at[5])
 
     def make_lists():
         for dx in (1, 3, 2):
@@ -123,11 +128,8 @@
         lies = (col // TD) % NC * HALF + col // (TD * NC) * TD + col % TD
         lists[4:5, :] = jnp.where(key < COL, lies, COL)
         lists[5:6, :] = lies
-        load = pltpu.make_async_copy(lists, table, in_s.at[5])
+        load = load_lists()
         load.start()
-        load.wait()
-        for dx in (1, 2, 3):
-            lcopy(dx).wait_send()
 
     far = [(j, 0, o) for j, o in enumerate(FAR)]
     near_own = [(4 + j, 0, o) for j, o in enumerate(NEAR)]
@@ -209,17 +211,12 @@
         def _():
             loads[1].wait()
             total_own()
-            t_first()
             loads[2].wait()
             for dx in (2, 1, 3):
                 ex(dx, x).start()
             make_lists()
 
         f_second()
-
-        @pl.when(r == 0)
-        def _():
-            t_second()
 
         f_third()
 
@@ -239,7 +236,24 @@
             f_close()
             to_core(c).wait_send()
 
+        def expect(tiles, at_row):
+            weights = jnp.concatenate([cb[at_row + k] for k in range(K)], axis=1)
+            return lax.dot_general(
+                jnp.concatenate(tiles, axis=1), weights, (((1,), (1,)), ((), ())),
+                preferred_element_type=jnp.float32,
+            )
+
+        def share(src_x, i, ratio):
+            row = src_x * LINKS + i * K
+            weights = jnp.concatenate([cb[row + k] for k in range(K)], axis=1)
+            got = jnp.dot(ratio, weights, preferred_element_type=jnp.float32)
+            for k in range(K):
+                sr[src_x * LINKS + k * CT + i] = got[:, k * TILE : (k + 1) * TILE].astype(
+                    jnp.bfloat16
+                )
+
         def by_tiles():
+            load_lists().wait()
             for dx in (2, 1, 3):
                 row = ((x + dx) % NX) * LINKS
 
@@ -256,6 +270,40 @@
 
             lax.fori_loop(0, LINKS, pick_own, 0, unroll=8)
 
+            t_first()
+            for dx in (1, 3, 2):
+                ex(dx, (x + NX - dx) % NX).wait_recv()
+                for dy in (2, 1, 3):
+                    ey(dx, dy, y).start()
+
+            def xwait(dx):
+                ref = xr.at[pl.ds(((x + NX - dx) % NX) * LINKS, LINKS)]
+                copy(ref, ref, fx_s.at[dx - 1], fx_r.at[dx - 1], at(dx=dx)).wait_recv()
+
+            for dx in (1, 3, 2):
+                xwait(dx)
+
+            def tile(i, _):
+                links = [k * CT + i for k in range(K)]
+                acc = expect(
+                    [xr[(tid[x * LINKS + l] // COL) * LINKS + l] for l in links], x * LINKS + i * K
+                )
+                ratio = (counts[:, pl.ds(pl.multiple_of(i * TILE, TILE), TILE)] / acc).astype(
+                    jnp.bfloat16
+                )
+                share(x, i, ratio)
+                return 0
+
+            lax.fori_loop(0, LINKS // K, tile, 0, unroll=2)
+
+            def scopy(dx, src_x):
+                ref = sr.at[pl.ds(src_x * LINKS, LINKS)]
+                return copy(ref, ref, rx_s.at[dx - 1], rx_r.at[dx - 1], at(dx=dx))
+
+            for dx in (2, 1, 3):
+                scopy(dx, x).start()
+            th_sent()
+            t_second()
             t_third()
             s = tt[0]
             for i in range(1, NZ):
@@ -264,50 +312,12 @@
             for j, (dx, dc) in enumerate(group):
                 tg(j, dx, dc).start()
             for dx in (1, 3, 2):
-                ex(dx, (x + NX - dx) % NX).wait_recv()
-                for dy in (2, 1, 3):
-                    ey(dx, dy, y).start()
-
-            def xwait(dx):
-                ref = xr.at[pl.ds(((x + NX - dx) % NX) * LINKS, LINKS)]
-                copy(ref, ref, fx_s.at[dx - 1], fx_r.at[dx - 1], at(dx=dx)).wait_recv()
-
-            for dx in (1, 3, 2):
-                xwait(dx)
-
-            def tile(i, _):
-                acc = jnp.zeros((16, TILE), jnp.float32)
-                for k in range(K):
-                    l = k * CT + i
-                    got = xr[(tid[x * LINKS + l] // COL) * LINKS + l]
-                    acc = acc + lax.dot_general(
-                        got, cb[x * LINKS + i * K + k], (((1,), (1,)), ((), ())),
-                        preferred_element_type=jnp.float32,
-                    )
-                ratio = (counts[:, pl.ds(pl.multiple_of(i * TILE, TILE), TILE)] / acc).astype(
-                    jnp.bfloat16
-                )
-                for k in range(K):
-                    sr[x * LINKS + k * CT + i] = jnp.dot(
-                        ratio, cb[x * LINKS + i * K + k], preferred_element_type=jnp.float32
-                    ).astype(jnp.bfloat16)
-                return 0
-
-            lax.fori_loop(0, LINKS // K, tile, 0, unroll=2)
-
-            def scopy(dx, src_x):
-                ref = sr.at[pl.ds(src_x * LINKS, LINKS)]
-                return copy(ref, ref, rx_s.at[dx - 1], rx_r.at[dx - 1], at(dx=dx))
-
-            for dx in (2, 1, 3):
-                scopy(dx, x).start()
-            th_sent()
-            for dx in (1, 3, 2):
                 scopy(dx, (x + NX - dx) % NX).wait_recv()
             for dx in (1, 2, 3):
                 xcopy(dx).wait_send()
                 scopy(dx, x).wait_send()
                 ex(dx, x).wait_send()
+                lcopy(dx).wait_send()
 
 
         def pcopy_x(dx):
@@ -331,13 +341,9 @@
                 row = ((x + dx) % NX) * LINKS
 
                 def part_sum(i, _, dx=dx, row=row):
-                    acc = jnp.zeros((16, TILE), jnp.float32)
-                    for k in range(K):
-                        acc = acc + lax.dot_general(
-                            th[mytile[row + k * CT + i]], cb[row + i * K + k],
-                            (((1,), (1,)), ((), ())), preferred_element_type=jnp.float32,
-                        )
-                    pe[dx * CT + i] = acc
+                    pe[dx * CT + i] = expect(
+                        [th[mytile[row + k * CT + i]] for k in range(K)], row + i * K
+                    )
                     return 0
 
                 lax.fori_loop(0, CT, part_sum, 0, unroll=4)
@@ -363,11 +369,7 @@
                     qcopy(dx, src_x).wait_recv()
 
                 def shares(i, _, src_x=src_x):
-                    for k in range(K):
-                        sr[src_x * LINKS + k * CT + i] = jnp.dot(
-                            rt[src_x * CT + i], cb[src_x * LINKS + i * K + k],
-                            preferred_element_type=jnp.float32,
-                        ).astype(jnp.bfloat16)
+                    share(src_x, i, rt[src_x * CT + i])
                     return 0
 
                 lax.fori_loop(0, CT, shares, 0, unroll=4)
@@ -391,31 +393,27 @@
 
         lax.fori_loop(0, COL, add, jnp.zeros((16, TILE), jnp.float32), unroll=8)
 
-        def dense(core):
-            def one(i, _):
+        def dense(core, off_sign, first, count):
+            for p in range(first, first + count):
+                zz = zs[off_sign * PLACES[p]]
                 for t in range(TD):
-                    g = (i * NC + core) * TD + t
-                    d[core * HALF + i * TD + t] = cum[pos[g]]
-                return 0
-
-            lax.fori_loop(0, NZ, one, 0, unroll=4)
-
-        dense(1 - c)
-        rcopy = copy(
-            d.at[pl.ds((1 - c) * HALF, HALF)], cr, rc_s.at[0], rc_r.at[0], at(dc=1)
-        )
-        rcopy.start()
-        dense(c)
-        rcopy.wait_recv()
-
-        def join(i, _):
-            d[c * HALF + i] = d[c * HALF + i] + cr[i]
-            return 0
-
-        lax.fori_loop(0, HALF, join, 0, unroll=8)
+                    d[core * HALF + p * TD + t] = cum[pos[(zz * NC + core) * TD + t]]
+
+        def rcopy(g):
+            first, count = GROUPS[g]
+            return copy(
+                d.at[pl.ds((1 - c) * HALF + first * TD, count * TD)],
+                cr.at[pl.ds(first * TD, count * TD)], rc_s.at[g], rc_r.at[g], at(dc=1),
+            )
+
+        for g, (first, count) in enumerate(GROUPS):
+            dense(1 - c, -1, first, count)
+            rcopy(g).start()
+        for first, count in GROUPS:
+            dense(c, 1, first, count)
 
         def dz(off):
-            return d.at[pl.ds(c * HALF + zrel(off) * TD, TD)]
+            return d.at[pl.ds(c * HALF + PLACES.index(off) * TD, TD)]
 
         kinds = (0,) + FAR
         nsteps = [
@@ -435,7 +433,11 @@
                 at(dz=way),
             )
 
-        for q in (1, 2, 3, 4):
+        for g, q in enumerate((1, 2, 3, 4, 0)):
+            rcopy(g).wait_recv()
+            first, count = GROUPS[g]
+            for i in range(first * TD, (first + count) * TD):
+                d[c * HALF + i] = d[c * HALF + i] + cr[i]
             for n in nsteps[q]:
                 ncopy(*n).start()
 
@@ -454,18 +456,15 @@
             for n in nsteps[q]:
                 ncopy(*n).wait_recv()
             for t in range(TD):
-                acc = d[c * HALF + zrel(kind) * TD + t]
+                acc = d[c * HALF + PLACES.index(kind) * TD + t]
                 for n in nsteps[q]:
                     acc = acc + nr[n[0] * TD + t]
                 sf[(q - 1) * TD + t] = acc
             fcopy(q - 1, kind).start()
-            if q == 2:
-                for n in nsteps[0]:
-                    ncopy(*n).start()
         for n in nsteps[0]:
             ncopy(*n).wait_recv()
         for t in range(TD):
-            acc = d[c * HALF + z * TD + t]
+            acc = d[c * HALF + PLACES.index(0) * TD + t]
             for n in nsteps[0]:
                 acc = acc + nr[n[0] * TD + t]
             sums[t] = acc
@@ -484,7 +483,8 @@
 
         for dy in (2, 1, 3):
             pcopy(dy).start()
-        rcopy.wait_send()
+        for g in range(len(GROUPS)):
+            rcopy(g).wait_send()
         for steps in nsteps:
             for n in steps:
                 ncopy(*n).wait_send()
@@ -551,7 +551,7 @@
             dma((1,)), dma((1,)),
             dma((3,)), dma((3,)),
             dma((3,)), dma((3,)),
-            dma((1,)), dma((1,)),
+            dma((5,)), dma((5,)),
             dma((11,)), dma((11,)),
             dma((4,)), dma((4,)),
             dma((15,)), dma((15,)),

time: 156 us -> 153 us (0.981)
  Pallas kernels: 154 us -> 150 us
    pallas_call x1, Pallas kernels: 154 us -> 150 us  [body(): pl.pallas_call(em_kernel, out_shape=jax.ShapeDtypeStruct(start.shape, f32...]
where the time goes in v5:
time: 153 us; the launch traced here: 151 us
  Pallas kernels  150 us (98%)
    pallas_call x1, Pallas kernels, body(): pl.pallas_call(em_kernel, out_shape=jax.ShapeDtypeStruct(start.shape, f32...  150 us

profile of v5, /device:TPU:1, one launch (start us, length us, event | category | flops | bytes accessed | tf_op | source)
XLA Modules:
  0.0 151.0 jit_solution(7875202622694383514)
XLA Ops:
  0.0 149.6 %em_rounds.1 = f32[16,512]{1,0:T(8,128)} custom-call(s32[4,8]{1,0:T(4,128)} %bitcast.4, s32[4,8]{1,0:T(4,128)} %bitcast.5, f32[16,1024]{1,0:T(8,128)} %counts_hbm.1, bf16[32,128,128]{2,1,0:T(8,128)(2,1)} %bitcast.3, f32[16,512]{1,0:T(8,128)} %start_hbm.1), custom_call_target="tpu_custom_call" | custom-call | tf_op jit(solution)/shard_map/em_rounds/pallas_call | solution.py:521
  149.6 1.4 copy.7

commit v6 on v5

--- a/solution.py
+++ b/solution.py
@@ -16,6 +16,8 @@
 TD = 4
 CT = 8
 LINKS = 32
+HALVES = 2
+PCT, PLINKS = CT // HALVES, LINKS // HALVES
 COL = NZ * NC * TD
 HALF = NZ * TD
 FAR = (6, -6, 3, -3)
@@ -26,11 +28,12 @@
 
 def em_kernel(
     owner_hbm, local_hbm, counts_hbm, compat_hbm, start_hbm, out,
-    owner, local, counts, cb, tab, raw, lists, table, th, xs, xr, sr, cum, d, cr, nr, sf, fr, tt, tx, tot, ps, theta,
+    owner, local, counts, cb, tab, raw, lists, table, th, xs, xr0, xr1, sr, cum, d, cr, nr, sf, fr, tt, tx, tot, ps, theta,
     fz_s, fz_r, fc_s, fc_r, fx_s, fx_r, rx_s, rx_r, rc_s, rc_r,
     rn_s, rn_r, rf_s, rf_r, tz_s, tz_r, tg_s, tg_r, p_s, p_r, l_s, l_r, in_s,
     sums, pe, pr, rt, ex_s, ex_r, ey_s, ey_r, pe_s, pe_r, q_s, q_r,
 ):
+    xr = (xr0, xr1)
     tid, perm, keep, pos, mytile, place = (table.at[i] for i in range(6))
     me = lax.axis_index("cls")
     y = lax.axis_index("smp")
@@ -82,15 +85,16 @@
     for load in loads:
         load.start()
     lane = lax.broadcasted_iota(jnp.int32, (8, TILE), 1)
-    raw[...] = jnp.zeros((8, TILE), jnp.int32)
+    level = lax.broadcasted_iota(jnp.int32, (8, TILE), 0)
     loads[3].wait()
     loads[4].wait()
+    raw[...] = jnp.zeros((8, TILE), jnp.int32)
     raw[0:K, 0:CT] = owner[...] * TD + local[...]
-    row = raw[0:1, :]
-    for k in range(1, K):
-        row = row + pltpu.roll(raw[k : k + 1, :], k * CT, 1)
-    for j in (1, 2):
-        row = row + pltpu.roll(row, j * LINKS, 1)
+    rows = jnp.zeros((8, TILE), jnp.int32)
+    for i in range(CT):
+        one = jnp.broadcast_to(raw[:, i : i + 1], (8, TILE))
+        rows = jnp.where((lane % LINKS // K == i) & (lane % K == level), one, rows)
+    row = jnp.sum(rows, axis=0, keepdims=True)
     tab[0] = jnp.where(lane // LINKS == x, jnp.broadcast_to(row, (8, TILE)), 0)
     pl.semaphore_wait(barrier, len(peers))
 
@@ -223,13 +227,11 @@
         to_core(c).start()
         to_core(1 - c).wait_recv()
 
-        def xcopy(dx):
+        def xcopy(dx, h):
+            j = (dx - 1) * HALVES + h
             return copy(
-                xs.at[pl.ds((dx - 1) * LINKS, LINKS)],
-                xr.at[pl.ds(x * LINKS, LINKS)],
-                fx_s.at[dx - 1],
-                fx_r.at[dx - 1],
-                at(dx=dx),
+                xs.at[pl.ds(j * PLINKS, PLINKS)], xr[h].at[pl.ds(x * PLINKS, PLINKS)],
+                fx_s.at[j], fx_r.at[j], at(dx=dx),
             )
 
         def th_sent():
@@ -248,27 +250,29 @@
             weights = jnp.concatenate([cb[row + k] for k in range(K)], axis=1)
             got = jnp.dot(ratio, weights, preferred_element_type=jnp.float32)
             for k in range(K):
-                sr[src_x * LINKS + k * CT + i] = got[:, k * TILE : (k + 1) * TILE].astype(
+                sr[src_x * LINKS + i * K + k] = got[:, k * TILE : (k + 1) * TILE].astype(
                     jnp.bfloat16
                 )
 
         def by_tiles():
             load_lists().wait()
-            for dx in (2, 1, 3):
-                row = ((x + dx) % NX) * LINKS
-
-                def pick(l, _, dx=dx, row=row):
-                    xs[(dx - 1) * LINKS + l] = th[place[row + l]]
+            for h in range(HALVES):
+                for dx in (2, 1, 3):
+                    row = ((x + dx) % NX) * LINKS + h * PLINKS
+
+                    def pick(l, _, base=((dx - 1) * HALVES + h) * PLINKS, row=row):
+                        xs[base + l] = th[place[row + l]]
+                        return 0
+
+                    lax.fori_loop(0, PLINKS, pick, 0, unroll=8)
+                    xcopy(dx, h).start()
+            for h in range(HALVES):
+
+                def pick_own(l, _, h=h):
+                    xr[h][x * PLINKS + l] = th[place[x * LINKS + h * PLINKS + l]]
                     return 0
 
-                lax.fori_loop(0, LINKS, pick, 0, unroll=8)
-                xcopy(dx).start()
-
-            def pick_own(l, _):
-                xr[x * LINKS + l] = th[place[x * LINKS + l]]
-                return 0
-
-            lax.fori_loop(0, LINKS, pick_own, 0, unroll=8)
+                lax.fori_loop(0, PLINKS, pick_own, 0, unroll=8)
 
             t_first()
             for dx in (1, 3, 2):
@@ -276,32 +280,34 @@
                 for dy in (2, 1, 3):
                     ey(dx, dy, y).start()
 
-            def xwait(dx):
-                ref = xr.at[pl.ds(((x + NX - dx) % NX) * LINKS, LINKS)]
-                copy(ref, ref, fx_s.at[dx - 1], fx_r.at[dx - 1], at(dx=dx)).wait_recv()
-
-            for dx in (1, 3, 2):
-                xwait(dx)
-
-            def tile(i, _):
-                links = [k * CT + i for k in range(K)]
-                acc = expect(
-                    [xr[(tid[x * LINKS + l] // COL) * LINKS + l] for l in links], x * LINKS + i * K
-                )
-                ratio = (counts[:, pl.ds(pl.multiple_of(i * TILE, TILE), TILE)] / acc).astype(
-                    jnp.bfloat16
-                )
-                share(x, i, ratio)
-                return 0
-
-            lax.fori_loop(0, LINKS // K, tile, 0, unroll=2)
-
-            def scopy(dx, src_x):
-                ref = sr.at[pl.ds(src_x * LINKS, LINKS)]
-                return copy(ref, ref, rx_s.at[dx - 1], rx_r.at[dx - 1], at(dx=dx))
-
-            for dx in (2, 1, 3):
-                scopy(dx, x).start()
+            def scopy(dx, h, src_x):
+                ref = sr.at[pl.ds(src_x * LINKS + h * PLINKS, PLINKS)]
+                j = (dx - 1) * HALVES + h
+                return copy(ref, ref, rx_s.at[j], rx_r.at[j], at(dx=dx))
+
+            for h in range(HALVES):
+                for dx in (1, 3, 2):
+                    ref = xr[h].at[pl.ds(((x + NX - dx) % NX) * PLINKS, PLINKS)]
+                    j = (dx - 1) * HALVES + h
+                    copy(ref, ref, fx_s.at[j], fx_r.at[j], at(dx=dx)).wait_recv()
+
+                def tile(n, _, h=h):
+                    i = h * PCT + n
+                    tiles = []
+                    for k in range(K):
+                        l = n * K + k
+                        src_x = tid[x * LINKS + h * PLINKS + l] // COL
+                        tiles.append(xr[h][src_x * PLINKS + l])
+                    acc = expect(tiles, x * LINKS + i * K)
+                    ratio = (counts[:, pl.ds(pl.multiple_of(i * TILE, TILE), TILE)] / acc).astype(
+                        jnp.bfloat16
+                    )
+                    share(x, i, ratio)
+                    return 0
+
+                lax.fori_loop(0, PCT, tile, 0, unroll=4)
+                for dx in (2, 1, 3):
+                    scopy(dx, h, x).start()
             th_sent()
             t_second()
             t_third()
@@ -311,24 +317,27 @@
             tx[0] = s
             for j, (dx, dc) in enumerate(group):
                 tg(j, dx, dc).start()
-            for dx in (1, 3, 2):
-                scopy(dx, (x + NX - dx) % NX).wait_recv()
+            for h in range(HALVES):
+                for dx in (1, 3, 2):
+                    scopy(dx, h, (x + NX - dx) % NX).wait_recv()
             for dx in (1, 2, 3):
-                xcopy(dx).wait_send()
-                scopy(dx, x).wait_send()
+                for h in range(HALVES):
+                    xcopy(dx, h).wait_send()
+                    scopy(dx, h, x).wait_send()
                 ex(dx, x).wait_send()
                 lcopy(dx).wait_send()
 
-
-        def pcopy_x(dx):
+        def pcopy_x(dx, h):
+            j = (dx - 1) * HALVES + h
             return copy(
-                pe.at[pl.ds(dx * CT, CT)], pr.at[pl.ds((dx - 1) * CT, CT)],
-                pe_s.at[dx - 1], pe_r.at[dx - 1], at(dx=dx),
+                pe.at[pl.ds(dx * CT + h * PCT, PCT)], pr.at[pl.ds((dx - 1) * CT + h * PCT, PCT)],
+                pe_s.at[j], pe_r.at[j], at(dx=dx),
             )
 
-        def qcopy(dx, src_x):
-            ref = rt.at[pl.ds(src_x * CT, CT)]
-            return copy(ref, ref, q_s.at[dx - 1], q_r.at[dx - 1], at(dx=dx))
+        def qcopy(dx, h, src_x):
+            ref = rt.at[pl.ds(src_x * CT + h * PCT, PCT)]
+            j = (dx - 1) * HALVES + h
+            return copy(ref, ref, q_s.at[j], q_r.at[j], at(dx=dx))
 
         def by_sums():
             @pl.when(r == 1)
@@ -337,45 +346,52 @@
                     for dy in (1, 2, 3):
                         ey(dx, dy, (y + NY - dy) % NY).wait_recv()
 
-            for dx in (2, 1, 3, 0):
-                row = ((x + dx) % NX) * LINKS
-
-                def part_sum(i, _, dx=dx, row=row):
-                    pe[dx * CT + i] = expect(
-                        [th[mytile[row + k * CT + i]] for k in range(K)], row + i * K
-                    )
-                    return 0
-
-                lax.fori_loop(0, CT, part_sum, 0, unroll=4)
-                if dx:
-                    pcopy_x(dx).start()
+            for h in range(HALVES):
+                for dx in (2, 1, 3, 0):
+                    row = ((x + dx) % NX) * LINKS
+
+                    def part_sum(i, _, dx=dx, row=row):
+                        pe[dx * CT + i] = expect(
+                            [th[mytile[row + i * K + k]] for k in range(K)], row + i * K
+                        )
+                        return 0
+
+                    lax.fori_loop(h * PCT, (h + 1) * PCT, part_sum, 0, unroll=4)
+                    if dx:
+                        pcopy_x(dx, h).start()
             th_sent()
-            for dx in (1, 3, 2):
-                pcopy_x(dx).wait_recv()
-
-            def ratio(i, _):
-                acc = pe[i] + pr[i] + pr[CT + i] + pr[2 * CT + i]
-                rt[x * CT + i] = (
-                    counts[:, pl.ds(pl.multiple_of(i * TILE, TILE), TILE)] / acc
-                ).astype(jnp.bfloat16)
-                return 0
-
-            lax.fori_loop(0, CT, ratio, 0, unroll=4)
-            for dx in (2, 1, 3):
-                qcopy(dx, x).start()
-            for dx in (0, 1, 3, 2):
-                src_x = (x + NX - dx) % NX
-                if dx:
-                    qcopy(dx, src_x).wait_recv()
-
-                def shares(i, _, src_x=src_x):
+
+            def shares(src_x, h):
+                def one(i, _):
                     share(src_x, i, rt[src_x * CT + i])
                     return 0
 
-                lax.fori_loop(0, CT, shares, 0, unroll=4)
+                lax.fori_loop(h * PCT, (h + 1) * PCT, one, 0, unroll=4)
+
+            for h in range(HALVES):
+                for dx in (1, 3, 2):
+                    pcopy_x(dx, h).wait_recv()
+
+                def ratio(i, _):
+                    acc = pe[i] + pr[i] + pr[CT + i] + pr[2 * CT + i]
+                    rt[x * CT + i] = (
+                        counts[:, pl.ds(pl.multiple_of(i * TILE, TILE), TILE)] / acc
+                    ).astype(jnp.bfloat16)
+                    return 0
+
+                lax.fori_loop(h * PCT, (h + 1) * PCT, ratio, 0, unroll=4)
+                for dx in (2, 1, 3):
+                    qcopy(dx, h, x).start()
+                shares(x, h)
+            for h in range(HALVES):
+                for dx in (1, 3, 2):
+                    src_x = (x + NX - dx) % NX
+                    qcopy(dx, h, src_x).wait_recv()
+                    shares(src_x, h)
             for dx in (1, 2, 3):
-                pcopy_x(dx).wait_send()
-                qcopy(dx, x).wait_send()
+                for h in range(HALVES):
+                    pcopy_x(dx, h).wait_send()
+                    qcopy(dx, h, x).wait_send()
 
             @pl.when(r == 1)
             def _():
@@ -534,7 +550,7 @@
             pltpu.SMEM((8, TILE), jnp.int32),
             buf(COL + 1, bf16),
             buf(3 * LINKS, bf16),
-            buf(NX * LINKS, bf16),
+            buf(NX * PLINKS, bf16), buf(NX * PLINKS, bf16),
             buf(NX * LINKS, bf16),
             buf(COL + 1, f32),
             buf(COL, f32),
@@ -549,8 +565,8 @@
             pltpu.VMEM((16, TD * TILE), f32),
             dma((15,)), dma((15,)),
             dma((1,)), dma((1,)),
-            dma((3,)), dma((3,)),
-            dma((3,)), dma((3,)),
+            dma((3 * HALVES,)), dma((3 * HALVES,)),
+            dma((3 * HALVES,)), dma((3 * HALVES,)),
             dma((5,)), dma((5,)),
             dma((11,)), dma((11,)),
             dma((4,)), dma((4,)),
@@ -564,8 +580,8 @@
             buf(NX * CT, bf16),
             dma((3,)), dma((3,)),
             dma((9,)), dma((9,)),
-            dma((3,)), dma((3,)),
-            dma((3,)), dma((3,)),
+            dma((3 * HALVES,)), dma((3 * HALVES,)),
+            dma((3 * HALVES,)), dma((3 * HALVES,)),
         ],
         compiler_params=pltpu.CompilerParams(
             collective_id=0, has_side_effects=True, vmem_limit_bytes=60 << 20

time: 153 us -> 149 us (0.974); the launches traced: 151 us -> 149 us
  Pallas kernels: 150 us -> 147 us
    pallas_call x1, Pallas kernels: 150 us -> 147 us  [body(): pl.pallas_call(em_kernel, out_shape=jax.ShapeDtypeStruct(start.shape, f32...]
where the time goes in v6:
time: 149 us
  Pallas kernels  147 us (99%)
    pallas_call x1, Pallas kernels, body(): pl.pallas_call(em_kernel, out_shape=jax.ShapeDtypeStruct(start.shape, f32...  147 us

profile of v6, /device:TPU:1, one launch (start us, length us, event | category | flops | bytes accessed | tf_op | source)
XLA Modules:
  0.0 148.6 jit_solution(217576086091961321)
XLA Ops:
  0.0 147.2 %em_rounds.1 = f32[16,512]{1,0:T(8,128)} custom-call(s32[4,8]{1,0:T(4,128)} %bitcast.4, s32[4,8]{1,0:T(4,128)} %bitcast.5, f32[16,1024]{1,0:T(8,128)} %counts_hbm.1, bf16[32,128,128]{2,1,0:T(8,128)(2,1)} %bitcast.3, f32[16,512]{1,0:T(8,128)} %start_hbm.1), custom_call_target="tpu_custom_call" | custom-call | tf_op jit(solution)/shard_map/em_rounds/pallas_call | solution.py:537
  147.2 1.4 copy.7

commit v7 on v6

--- a/solution.py
+++ b/solution.py
@@ -195,11 +195,16 @@
     def tg(j, dx, dc):
         return copy(tx.at[0], tx.at[1 + j], tg_s.at[j], tg_r.at[j], at(dx=dx, dc=dc))
 
-    part = LINKS // NY
-
-    def ex(dx, src_x):
-        ref = cb.at[pl.ds(src_x * LINKS + y * part, part)]
-        return copy(ref, ref, ex_s.at[dx - 1], ex_r.at[dx - 1], at(dx=dx))
+    part = 6
+    rest = LINKS - NY * part
+
+    def ex(dx, src_x, step):
+        if step < 2:
+            ref = cb.at[pl.ds(src_x * LINKS + (y + 2 * step) % NY * part, part)]
+        else:
+            ref = cb.at[pl.ds(src_x * LINKS + NY * part, rest)]
+        j = step * 3 + dx - 1
+        return copy(ref, ref, ex_s.at[j], ex_r.at[j], at(dx=dx))
 
     def ey(dx, dy, src_y):
         ref = cb.at[pl.ds(((x + NX - dx) % NX) * LINKS + src_y * part, part)]
@@ -217,7 +222,7 @@
             total_own()
             loads[2].wait()
             for dx in (2, 1, 3):
-                ex(dx, x).start()
+                ex(dx, x, 0).start()
             make_lists()
 
         f_second()
@@ -276,8 +281,8 @@
 
             t_first()
             for dx in (1, 3, 2):
-                ex(dx, (x + NX - dx) % NX).wait_recv()
-                for dy in (2, 1, 3):
+                ex(dx, (x + NX - dx) % NX, 0).wait_recv()
+                for dy in (1, 3):
                     ey(dx, dy, y).start()
 
             def scopy(dx, h, src_x):
@@ -324,7 +329,7 @@
                 for h in range(HALVES):
                     xcopy(dx, h).wait_send()
                     scopy(dx, h, x).wait_send()
-                ex(dx, x).wait_send()
+                ex(dx, x, 0).wait_send()
                 lcopy(dx).wait_send()
 
         def pcopy_x(dx, h):
@@ -343,7 +348,9 @@
             @pl.when(r == 1)
             def _():
                 for dx in (1, 2, 3):
-                    for dy in (1, 2, 3):
+                    ex(dx, (x + NX - dx) % NX, 1).wait_recv()
+                    ex(dx, (x + NX - dx) % NX, 2).wait_recv()
+                    for dy in (1, 3):
                         ey(dx, dy, (y + NY - dy) % NY).wait_recv()
 
             for h in range(HALVES):
@@ -396,7 +403,9 @@
             @pl.when(r == 1)
             def _():
                 for dx in (1, 2, 3):
-                    for dy in (1, 2, 3):
+                    ex(dx, x, 1).wait_send()
+                    ex(dx, x, 2).wait_send()
+                    for dy in (1, 3):
                         ey(dx, dy, y).wait_send()
 
         pl.when(r == 0)(by_tiles)
@@ -477,6 +486,12 @@
                     acc = acc + nr[n[0] * TD + t]
                 sf[(q - 1) * TD + t] = acc
             fcopy(q - 1, kind).start()
+        @pl.when(r == 0)
+        def _():
+            for dx in (2, 1, 3):
+                ex(dx, x, 1).start()
+                ex(dx, x, 2).start()
+
         for n in nsteps[0]:
             ncopy(*n).wait_recv()
         for t in range(TD):
@@ -578,7 +593,7 @@
             buf(NX * CT, f32),
             buf(3 * CT, f32),
             buf(NX * CT, bf16),
-            dma((3,)), dma((3,)),
+            dma((9,)), dma((9,)),
             dma((9,)), dma((9,)),
             dma((3 * HALVES,)), dma((3 * HALVES,)),
             dma((3 * HALVES,)), dma((3 * HALVES,)),

time: 149 us -> 144 us (0.966)
  Pallas kernels: 147 us -> 142 us
    pallas_call x1, Pallas kernels: 147 us -> 142 us  [body(): pl.pallas_call(em_kernel, out_shape=jax.ShapeDtypeStruct(start.shape, f32...]
where the time goes in v7:
time: 144 us
  Pallas kernels  142 us (99%)
    pallas_call x1, Pallas kernels, body(): pl.pallas_call(em_kernel, out_shape=jax.ShapeDtypeStruct(start.shape, f32...  142 us

profile of v7, /device:TPU:1, one launch (start us, length us, event | category | flops | bytes accessed | tf_op | source)
XLA Modules:
  0.0 143.7 jit_solution(3839899781124222145)
XLA Ops:
  0.0 142.3 %em_rounds.1 = f32[16,512]{1,0:T(8,128)} custom-call(s32[4,8]{1,0:T(4,128)} %bitcast.4, s32[4,8]{1,0:T(4,128)} %bitcast.5, f32[16,1024]{1,0:T(8,128)} %counts_hbm.1, bf16[32,128,128]{2,1,0:T(8,128)(2,1)} %bitcast.3, f32[16,512]{1,0:T(8,128)} %start_hbm.1), custom_call_target="tpu_custom_call" | custom-call | tf_op jit(solution)/shard_map/em_rounds/pallas_call | solution.py:552
  142.3 1.4 copy.7

commit v8 on v7

--- a/solution.py
+++ b/solution.py
@@ -354,7 +354,7 @@
                         ey(dx, dy, (y + NY - dy) % NY).wait_recv()
 
             for h in range(HALVES):
-                for dx in (2, 1, 3, 0):
+                for dx in (2, 1, 3) + ((0,) if h == HALVES - 1 else ()):
                     row = ((x + dx) % NX) * LINKS
 
                     def part_sum(i, _, dx=dx, row=row):
@@ -363,7 +363,7 @@
                         )
                         return 0
 
-                    lax.fori_loop(h * PCT, (h + 1) * PCT, part_sum, 0, unroll=4)
+                    lax.fori_loop(h * PCT if dx else 0, (h + 1) * PCT, part_sum, 0, unroll=4)
                     if dx:
                         pcopy_x(dx, h).start()
             th_sent()

time: 144 us -> 144 us (level)
  no operation moved by 1% of the time
where the time goes in v8:
time: 144 us; the launch traced here: 143 us
  Pallas kernels  142 us (99%)
    pallas_call x1, Pallas kernels, body(): pl.pallas_call(em_kernel, out_shape=jax.ShapeDtypeStruct(start.shape, f32...  142 us

profile of v8, /device:TPU:1, one launch (start us, length us, event | category | flops | bytes accessed | tf_op | source)
XLA Modules:
  0.0 142.9 jit_solution(16810724384705095131)
XLA Ops:
  0.0 141.5 %em_rounds.1 = f32[16,512]{1,0:T(8,128)} custom-call(s32[4,8]{1,0:T(4,128)} %bitcast.4, s32[4,8]{1,0:T(4,128)} %bitcast.5, f32[16,1024]{1,0:T(8,128)} %counts_hbm.1, bf16[32,128,128]{2,1,0:T(8,128)(2,1)} %bitcast.3, f32[16,512]{1,0:T(8,128)} %start_hbm.1), custom_call_target="tpu_custom_call" | custom-call | tf_op jit(solution)/shard_map/em_rounds/pallas_call | solution.py:552
  141.5 1.4 copy.7

commit v9 on v7

--- a/solution.py
+++ b/solution.py
@@ -428,7 +428,7 @@
             first, count = GROUPS[g]
             return copy(
                 d.at[pl.ds((1 - c) * HALF + first * TD, count * TD)],
-                cr.at[pl.ds(first * TD, count * TD)], rc_s.at[g], rc_r.at[g], at(dc=1),
+                cr.at[pl.ds(first * TD, count * TD)], rc_s.at[0], rc_r.at[g], at(dc=1),
             )
 
         for g, (first, count) in enumerate(GROUPS):
@@ -449,12 +449,12 @@
 
         def ncopy(slot, way, dest):
             return copy(
-                dz(dest), nr.at[pl.ds(slot * TD, TD)], rn_s.at[slot], rn_r.at[slot], at(dz=way)
+                dz(dest), nr.at[pl.ds(slot * TD, TD)], rn_s.at[0], rn_r.at[slot], at(dz=way)
             )
 
         def fcopy(j, way):
             return copy(
-                sf.at[pl.ds(j * TD, TD)], fr.at[pl.ds(j * TD, TD)], rf_s.at[j], rf_r.at[j],
+                sf.at[pl.ds(j * TD, TD)], fr.at[pl.ds(j * TD, TD)], rf_s.at[0], rf_r.at[j],
                 at(dz=way),
             )
 
@@ -514,13 +514,8 @@
 
         for dy in (2, 1, 3):
             pcopy(dy).start()
-        for g in range(len(GROUPS)):
-            rcopy(g).wait_send()
-        for steps in nsteps:
-            for n in steps:
-                ncopy(*n).wait_send()
-        for j, way in enumerate(FAR):
-            fcopy(j, way).wait_send()
+        for ref, sem in ((cr, rc_s), (nr, rn_s), (fr, rf_s)):
+            copy(ref, ref, sem.at[0], sem.at[0], at(dc=1)).wait_send()
 
         @pl.when(r == 0)
         def _():

time: 144 us -> 145 us (level)
  no operation moved by 1% of the time
where the time goes in v9:
time: 145 us
  Pallas kernels  143 us (99%)
    pallas_call x1, Pallas kernels, body(): pl.pallas_call(em_kernel, out_shape=jax.ShapeDtypeStruct(start.shape, f32...  143 us

profile of v9, /device:TPU:1, one launch (start us, length us, event | category | flops | bytes accessed | tf_op | source)
XLA Modules:
  0.0 144.9 jit_solution(8062689727931131121)
XLA Ops:
  0.0 143.5 %em_rounds.1 = f32[16,512]{1,0:T(8,128)} custom-call(s32[4,8]{1,0:T(4,128)} %bitcast.4, s32[4,8]{1,0:T(4,128)} %bitcast.5, f32[16,1024]{1,0:T(8,128)} %counts_hbm.1, bf16[32,128,128]{2,1,0:T(8,128)(2,1)} %bitcast.3, f32[16,512]{1,0:T(8,128)} %start_hbm.1), custom_call_target="tpu_custom_call" | custom-call | tf_op jit(solution)/shard_map/em_rounds/pallas_call | solution.py:547
  143.5 1.4 copy.7
